TPU v7x, 512 devices: a whole 4x8x8 slice. The times are simulated.
512 devices in a mesh: atom: 128 (over y, z_hi, x, core), mode: 4 (over z_lo).
Axes of the slice: x: 4, y: 8, z: 8 (z_hi: 2, z_lo: 4; z = z_hi * 4 + z_lo), core: 2. Of those that a mesh axis runs over, the one named last changes fastest.
Arguments:
- velocity: bfloat16 [196608, 128], P('atom'), may hold values from -6 to 6
- local_virial: bfloat16 [196608, 384], P('atom'), may hold values from -6 to 6
- ghost_virial: bfloat16 [49152, 384], P('atom'), may hold values from -6 to 6
- eigvec: bfloat16 [196608, 4096], P('atom', 'mode'), may hold values from -0.0546875 to 0.0546875
- ghost_slot: int32 [16384], P('atom'), may hold values from 0 to 127, as said below
- counts: int32 [128], P('atom'), may hold values from 128 to 512, as said below
Outputs:
- modal_current: float32 [4, 1024, 3, 128], P('mode', 'atom')
- modal_corr: float32 [4, 1024, 64], P('mode', 'atom')
- slab_corr: float32 [64], replicated
Inputs may be any that keep to these rules, and one draw needn't show every extreme that they name: `ghost_slot`: for each domain the first 64 ghost slots are a permutation of 64 to 127 and the last 64 a permutation of 0 to 63. `counts`: every draw has a domain with 512 atoms and one with 128.
All inputs are finite; a program needn't handle non-finite values.
Results may differ from a plain program's by a relative error of at most 0.0003.
Values may be sent and summed in bfloat16 or wider, within the bound.
A program may use at most 64 MiB of HBM per device.

v0:
```python
import math

import jax
import jax.numpy as jnp
from jax import lax
from jax.sharding import PartitionSpec as P


def shifted(shard, axis, by):
    length = lax.axis_size(axis)
    return lax.ppermute(shard, axis, [(i, (i + by) % length) for i in range(length)])


def align_face(ghost_rows, slots, face_size):
    target = jnp.arange(face_size, dtype=jnp.int32)
    onehot = (slots[None, :] == target[:, None]).astype(jnp.bfloat16)
    shaped = ghost_rows.reshape(face_size, 3, ghost_rows.shape[1])
    placed = jnp.einsum("sg,gac->sac", onehot, shaped, preferred_element_type=jnp.float32)
    return placed.astype(jnp.bfloat16).reshape(3 * face_size, ghost_rows.shape[1])


def contract_rows(left_side, right_side):
    return lax.dot_general(
        left_side, right_side, (((0,), (0,)), ((), ())), preferred_element_type=jnp.float32
    )


def per_device(velocity, local_virial, ghost_virial, eigvec, ghost_slot, counts):
    frames = velocity.shape[1]
    slot_rows = velocity.shape[0]
    block_modes = eigvec.shape[1]
    face_size = ghost_slot.shape[0] // 2
    face_rows = 3 * face_size
    domains = lax.axis_size("atom")
    mode_share = block_modes // domains
    lag_count = frames // 2
    alive_rows = (jnp.arange(slot_rows, dtype=jnp.int32) // 3 < counts[0]).astype(jnp.bfloat16)[
        :, None
    ]
    moving = velocity * alive_rows
    stress = local_virial * alive_rows
    owned_below = align_face(
        ghost_virial[:face_rows], ghost_slot[:face_size] - face_size, face_size
    )
    owned_above = align_face(ghost_virial[face_rows:], ghost_slot[face_size:], face_size)
    got_lower = shifted(owned_above, "atom", 1)
    got_upper = shifted(owned_below, "atom", -1)
    ghost_rows = jnp.concatenate([got_lower, got_upper], axis=0)
    face_modes = eigvec[: 2 * face_rows]
    face_speed = velocity[: 2 * face_rows]
    speeds = contract_rows(eigvec, moving)
    loads = contract_rows(eigvec, stress) + contract_rows(face_modes, ghost_rows)
    summed = lax.psum(jnp.concatenate([speeds, loads], axis=1), "atom")
    owned_share = lax.dynamic_slice_in_dim(
        summed, lax.axis_index("atom") * mode_share, mode_share, 0
    )
    speed_part = owned_share[:, :frames]
    virial_part = owned_share[:, frames:].reshape(mode_share, 3, frames)
    modal_flux = speed_part[:, None, :] * virial_part
    stress_three = stress.reshape(slot_rows, 3, frames)
    current_part = jnp.einsum(
        "rbt,rt->bt", stress_three, moving, preferred_element_type=jnp.float32
    )
    ghost_three = ghost_rows.reshape(2 * face_rows, 3, frames)
    current_part = current_part + jnp.einsum(
        "rbt,rt->bt", ghost_three, face_speed, preferred_element_type=jnp.float32
    )
    current_sum = lax.psum(current_part, "atom") / math.sqrt(slot_rows // 3 * domains)
    padded = jnp.concatenate([current_sum, jnp.zeros((3, lag_count), jnp.float32)], axis=1)
    lag_index = (
        jnp.arange(frames, dtype=jnp.int32)[:, None]
        + jnp.arange(lag_count, dtype=jnp.int32)[None, :]
    )
    hankel = padded[:, lag_index]
    lag_corr = jnp.einsum("nbt,btl->nl", modal_flux, hankel, precision=lax.Precision.HIGHEST)
    lag_corr = lag_corr / (frames - jnp.arange(lag_count)).astype(jnp.float32)[None, :]
    all_modes = block_modes * lax.axis_size("mode")
    slab_sum = lax.psum(jnp.sum(lag_corr, axis=0), ("atom", "mode")) / math.sqrt(all_modes)
    return (modal_flux[None], lag_corr[None], slab_sum)


def solution(mesh):
    return jax.shard_map(
        per_device,
        mesh=mesh,
        in_specs=(
            P("atom", None),
            P("atom", None),
            P("atom", None),
            P("atom", "mode"),
            P("atom"),
            P("atom"),
        ),
        out_specs=(P("mode", "atom", None, None), P("mode", "atom", None), P()),
        check_vma=False,
    )
```

profile of v0, /device:TPU:1, one launch (start us, length us, event | category | flops | bytes accessed | tf_op | source)
XLA Modules:
  0.0 1717.6 jit_solution(1344348338189095907)
XLA Ops:
  7.2 0.8 slice_add_fusion
  8.0 1.0 fusion.24
  9.4 0.8 reshape.90
  10.2 8.8 collective-permute-start.1
  19.4 0.8 reshape.88
  20.2 1.9 collective-permute-start
  22.7 2.6 copy.14
  25.3 1.4 broadcast_multiply_fusion
  26.7 2.6 fusion.26
  29.3 1.8 convolution_bitcast_fusion
  31.7 1.5 reshape.97
  33.3 0.9 constant_dynamic-update-slice_fusion.1
  34.2 0.9 constant_dynamic-update-slice_fusion
  35.9 2.1 add_bitcast_fusion
  37.9 1.5 pad_maximum_fusion
  40.7 2.2 fusion
  43.8 807.7 %psum.22 = f32[3,128]{0,1:T(8,128)S(1)} all-reduce(f32[3,128]{0,1:T(8,128)S(1)} %add_bitcast_fusion.1), channel_id=1, replica_groups=mesh['atom'=128,'mode'=4] {'atom'}, use_global_device_ids=true, to_apply=%region_1.2 | all-reduce | flops 384 | bytes 3072 | tf_op jit(solution)/shard_map/psum | solution.py:68
  851.5 27.8 %gather_fusion = f32[8192,3]{1,0:T(8,128)} fusion(f32[3,192]{0,1:T(8,128)S(1)} %concatenate.11, s32[8192]{0:T(1024)S(1)} %broadcast_clamp_fusion), kind=kCustom, calls=%fused_computation | custom fusion | bytes 229376 | tf_op jit(solution)/shard_map/gather | solution.py:74
  879.3 3.7 copy.24
  883.1 722.2 %all-reduce.3.cloned.1.call-done = f32[1024,512]{0,1:T(8,128)} async-done(((f32[1024,512]{0,1:T(8,128)}), f32[1024,512]{0,1:T(8,128)}) %all-reduce.3.cloned.1.call-update) | async-done | bytes 2097168 | tf_op jit(solution)/shard_map/psum | solution.py:53
  1605.3 0.9 constant_dynamic-slice_fusion
  1606.2 1.1 dynamic-slice.1
  1608.1 0.8 fusion.25
  1608.9 101.3 %psum.23 = f32[64]{0:T(128)S(1)} all-reduce(f32[64]{0:T(128)S(1)} %get-tuple-element.7), channel_id=1, replica_groups=mesh['atom'=128,'mode'=4] {'atom','mode'}, use_global_device_ids=true, to_apply=%region_3.4 | all-reduce | flops 64 | bytes 512 | tf_op jit(solution)/shard_map/psum | solution.py:78
  (44 shorter events, 5.7 us)
Async XLA Ops:
  7.2 1598.1 %all-reduce.3.cloned.1.call-start = ((), (), s32[]{:S(2)}) async-start(), calls=%async_computation | async-start | bytes 4194304 | tf_op jit(solution)/shard_map/psum | solution.py:53
  10.2 24.0 %collective-permute-start.1 = (bf16[192,384]{1,0:T(8,128)(2,1)}, bf16[192,384]{1,0:T(8,128)(2,1)}, u32[]{:S(2)}, u32[]{:S(2)}) collective-permute-start(bf16[192,384]{1,0:T(8,128)(2,1)} %reshape.90), channel_id=1, source_target_pairs={{0,508},{4,0},{8,4},{12,8},{16,12},{20,16},{24,20},{28,24},{32,28}... | collective-permute-start | bytes 442376 | tf_op jit(solution)/shard_map/ppermute | solution.py:11
  20.2 13.1 collective-permute-start
  22.7 3.9 copy-start
  26.7 2.6 copy-start.5
  26.7 2.6 copy-start.2
  35.1 0.7 copy-start.3
  35.9 2.1 copy-start.1
  39.4 1.2 copy-start.7
  39.4 1.3 copy-start.6
  40.7 2.2 copy-start.4
Sparse Core Ops, SparseCore 0:
  39.5 1565.6 all-reduce.2
where the time goes:
time: 1720 us
  blocking collectives  909 us (53%)
  waiting for transfers between devices  722 us (42%)
  local copies, waits for them, and re-layouts  44.6 us (3%)
    psum x1, blocking collectives, per_device(): lax.psum(current_part, 'atom') / math.sqrt(slot_rows // 3 * domains)  808 us
    psum x1, waiting for transfers between devices, per_device(): summed = lax.psum(jnp.concatenate([speeds, loads], axis=1), 'atom')  722 us
    psum x1, blocking collectives, per_device(): lax.psum(jnp.sum(lag_corr, axis=0), ('atom', 'mode')) / math.sqrt(all_modes)  101 us
  transfers between devices with their start and end apart: 3, of which 1 were waited for; matrix products, arithmetic and copies ran while one was open for 3% of the time, Pallas kernels for 0%

commit v1 on v0

v1 whole, which is shorter than its diff:
```python
import functools
import math

import jax
import jax.numpy as jnp
from jax import lax
from jax.experimental import pallas as pl
from jax.experimental.pallas import tpu as pltpu
from jax.sharding import PartitionSpec as P

MESH = pl.DeviceIdType.MESH
F32 = jnp.float32
BF16 = jnp.bfloat16
HIGHEST = lax.Precision.HIGHEST
NY, NH, NX, NC, NM = 8, 2, 4, 2, 4
T = 128
K = 8
FACE = 192
LAGS = 64


def dot_rows(left, right):
    return lax.dot_general(left, right, (((0,), (0,)), ((), ())), preferred_element_type=F32)


def iota(shape, dim):
    return lax.broadcasted_iota(jnp.int32, shape, dim)


def placing(slots, face):
    ghost = iota((T, FACE), 0) - 64 * face
    third = lax.shift_right_logical(iota((T, FACE), 1) * 171, 9)
    spread = jnp.where(ghost == third, 1.0, 0.0).astype(BF16)
    base = 64 if face == 0 else 0
    slot = (slots - base).astype(F32).astype(BF16)
    slot = jnp.dot(jnp.broadcast_to(slot, (8, T)), spread, preferred_element_type=F32)
    lane = iota((8, FACE), 1)
    third = lax.shift_right_logical(lane * 171, 9)
    target = 3 * slot.astype(jnp.int32) + (lane - 3 * third)
    return jnp.where(iota((FACE, FACE), 0) == target[0:1, :], 1.0, 0.0).astype(BF16)


def hankel(total):
    parts = []
    for b in range(3):
        row = jnp.concatenate([total[b : b + 1, :], jnp.zeros((1, T), F32)], axis=1)
        row = jnp.broadcast_to(row, (T, 2 * T))
        parts.append(pltpu.roll(row, T + 1, 1, stride=1, stride_axis=0)[:, :T])
    flipped = jnp.concatenate(parts, axis=1)
    flip = jnp.where(iota((T, T), 0) + iota((T, T), 1) == T - 1, 1.0, 0.0).astype(F32)
    return jnp.dot(flip, flipped, precision=HIGHEST, preferred_element_type=F32)


def correlate(parts, lagged):
    out = None
    for b in range(3):
        term = jnp.dot(
            parts[b], lagged[:, b * T : (b + 1) * T], precision=HIGHEST, preferred_element_type=F32
        )
        out = term if out is None else out + term
    return out / (T - iota(out.shape, 1)).astype(F32)


def kernel(
    vel, vir, gho, eig, slots, counts, flux_out, corr_out, slab_out,
    ev, ms, gv, sv, placed, gh, part, cr, cs, ry, rx, x1, ry2, y1, rx2, zz, rh,
    tp, tc, tx, ty, th, sz, sy, sx,
    load_sem, gh_s, gh_r, c_s, c_r, rx_s, rx_r, ry_s, ry_r, ry2_s, ry2_r, rx2_s, rx2_r, h_s, h_r,
    t_s, t_r, sz_s, sz_r, sy_s, sy_r, sx_s, sx_r,
):
    a = lax.axis_index("atom")
    m = lax.axis_index("mode")
    c, x, h, y = lax.rem(a, 2), lax.rem(lax.div(a, 2), 4), lax.rem(lax.div(a, 8), 2), lax.div(a, 16)
    place = lax.rem(a, 8)

    def dev(y=y, h=h, x=x, c=c, m=m):
        return (((y * NH + h) * NX + x) * NC + c, m)

    core = dev(c=1 - c)
    x_peers = [lax.rem(x + k, NX) for k in range(1, NX)]
    y_peers = [lax.rem(y + k, NY) for k in range(1, NY)]
    z_peers = [
        (lax.rem(h + i // 8, NH), lax.rem(m + (i // 2) % 4, NM), lax.rem(c + i % 2, NC))
        for i in range(1, 16)
    ]
    h_peer = dev(h=1 - h)
    domains = NY * NH * NX * NC
    above, below = lax.rem(a + 1, domains), lax.rem(a + domains - 1, domains)
    up_far, down_far = place == 7, place == 0
    edge = jnp.logical_or(m == 0, m == 3)
    far_source = jnp.where(m < 2, 3, 0)
    far_first = jnp.where(m == 3, 0, 2)

    loads = [
        pltpu.make_async_copy(slots, sv, load_sem.at[0]),
        pltpu.make_async_copy(gho, gv, load_sem.at[1]),
        pltpu.make_async_copy(vel, ms.at[:, 0:T], load_sem.at[2]),
        pltpu.make_async_copy(vir, ms.at[:, T:], load_sem.at[3]),
    ]
    loads += [
        pltpu.make_async_copy(
            eig.at[pl.ds(192 * i, 192)], ev.at[pl.ds(192 * i, 192)], load_sem.at[4 + i]
        )
        for i in range(8)
    ]

    barrier = pltpu.get_barrier_semaphore()

    def greet(device):
        pl.semaphore_signal(barrier, 1, device_id=device, device_id_type=MESH)

    greet((below, jnp.where(down_far, far_source, m)))
    greet((above, jnp.where(up_far, far_source, m)))
    for xx in x_peers:
        greet(dev(x=xx))
    for yy in y_peers:
        greet(dev(y=yy))
    for hh, mm, cc in z_peers:
        greet(dev(h=hh, m=mm, c=cc))
    for load in loads:
        load.start()

    def ghost_sends():
        for side, (far, there) in enumerate(((up_far, above), (down_far, below))):
            first = jnp.where(far, far_first, m)
            once = jnp.logical_or(jnp.logical_not(far), edge)
            twice = jnp.logical_and(far, edge)
            for n, (when, mode) in enumerate(((once, first), (twice, far_first + 1))):
                yield when, pltpu.make_async_remote_copy(
                    src_ref=placed.at[side],
                    dst_ref=gh.at[side],
                    send_sem=gh_s.at[side, n],
                    recv_sem=gh_r.at[side],
                    device_id=(there, mode),
                    device_id_type=MESH,
                )

    sends = []

    def put(src, dst, send_sem, recv_sem, device):
        copy = pltpu.make_async_remote_copy(
            src_ref=src, dst_ref=dst, send_sem=send_sem, recv_sem=recv_sem,
            device_id=device, device_id_type=MESH,
        )
        copy.start()
        sends.append(copy)

    def arrived(dst, send_sem, recv_sem):
        pltpu.make_async_remote_copy(
            src_ref=dst, dst_ref=dst, send_sem=send_sem, recv_sem=recv_sem,
            device_id=core, device_id_type=MESH,
        ).wait_recv()

    loads[0].wait()
    loads[1].wait()
    for face in range(2):
        rows = jnp.dot(
            placing(sv[...], face), gv[FACE * face : FACE * (face + 1), :], preferred_element_type=F32
        )
        placed[1 - face] = rows.astype(BF16)
    sent_ghosts = 2 * jnp.ones((), jnp.int32)
    far = jnp.logical_or(up_far, down_far)
    sent_ghosts = jnp.where(far, jnp.where(edge, 3, 1), 2)
    pl.semaphore_wait(barrier, 3 + 7 + 15 + sent_ghosts)
    for when, copy in ghost_sends():
        pl.when(when)(copy.start)

    for load in loads[2:4]:
        load.wait()
    alive = jnp.where(iota((ms.shape[0], T), 0) < 3 * counts[0], 1.0, 0.0).astype(BF16)
    for q in range(4):
        ms[:, q * T : (q + 1) * T] = ms[:, q * T : (q + 1) * T] * alive
    for load in loads[4:]:
        load.wait()
    order = [lax.rem(lax.div(y, 2) + k, 4) for k in (1, 2, 3, 0)]
    for j in order:
        cols = pl.ds(pl.multiple_of(j * 256, 256), 256)
        acc = dot_rows(ev[:, cols], ms[...])
        for q in range(4):
            part[q, pl.ds(2 * j, 2)] = acc[:, q * T : (q + 1) * T].reshape(2, NH, NX, NC, K, T)
    total = dot_rows(ms[:, :T], ms[:, T:])

    for side in range(2):
        arrived(gh.at[side], gh_s.at[side, 0], gh_r.at[side])
    ghosts = gh[...].reshape(2 * FACE, 3 * T)
    total = total + dot_rows(ms[: 2 * FACE, :T], ghosts)
    diagonal = iota((T, T), 0) == iota((T, T), 1)
    tp[...] = jnp.concatenate(
        [
            jnp.sum(jnp.where(diagonal, total[:, b * T : (b + 1) * T], 0.0), axis=0, keepdims=True)
            for b in range(3)
        ]
        + [jnp.zeros((5, T), F32)],
        axis=0,
    )
    put(tp, tc, t_s.at[0], t_r.at[0], core)
    for k, j in enumerate(order):
        cols = pl.ds(pl.multiple_of(j * 256, 256), 256)
        acc = dot_rows(ev[: 2 * FACE, cols], ghosts)
        for q in range(1, 4):
            now = acc[:, (q - 1) * T : q * T].reshape(2, NH, NX, NC, K, T)
            part[q, pl.ds(2 * j, 2)] = part[q, pl.ds(2 * j, 2)] + now
        put(
            part.at[:, pl.ds(2 * j, 2), :, :, 1 - c], cr.at[:, pl.ds(2 * j, 2)],
            c_s.at[k], c_r.at[k], core,
        )

    arrived(tc, t_s.at[0], t_r.at[0])
    tx[x] = tp[...] + tc[...]
    for k, xx in enumerate(x_peers):
        put(tx.at[x], tx.at[x], t_s.at[1 + k], t_r.at[1 + x], dev(x=xx))
    for k, j in enumerate(order):
        two = pl.ds(2 * j, 2)
        arrived(cr.at[:, two], c_s.at[k], c_r.at[k])
        cs[:, two] = part[:, two, :, :, c] + cr[:, two]
        for n, xx in enumerate(x_peers):
            put(cs.at[2:4, two, :, xx], rx.at[n, :, two], rx_s.at[n, k], rx_r.at[n, k], dev(x=xx))
        targets = [2 * j, 2 * j + 1] if k < 3 else [y + 1 - 2 * lax.rem(y, 2)]
        for n, yy in enumerate(targets):
            put(cs.at[0:2, yy], ry.at[y], ry_s.at[2 * k + n], ry_r.at[y], dev(y=yy))
    for xx in x_peers:
        arrived(tx.at[xx], t_s.at[0], t_r.at[1 + xx])
    ty[y] = ((tx[0] + tx[1]) + tx[2]) + tx[3]
    for k, yy in enumerate(y_peers):
        put(ty.at[y], ty.at[y], t_s.at[4 + k], t_r.at[5 + y], dev(y=yy))
    for k, j in enumerate(order):
        two = pl.ds(2 * j, 2)
        for n in range(3):
            arrived(rx.at[n, :, two], rx_s.at[n, k], rx_r.at[n, k])
        x1[:, two] = (cs[2:4, two, :, x] + rx[0, :, two]) + (rx[1, :, two] + rx[2, :, two])
        targets = [2 * j, 2 * j + 1] if k < 3 else [y + 1 - 2 * lax.rem(y, 2)]
        for n, yy in enumerate(targets):
            put(x1.at[:, yy], ry2.at[y], ry2_s.at[2 * k + n], ry2_r.at[y], dev(y=yy))
    summed = cs[0:2, y]
    for yy in y_peers:
        arrived(ry.at[yy], ry_s.at[0], ry_r.at[yy])
        summed = summed + ry[yy]
    y1[...] = summed
    for n, xx in enumerate(x_peers):
        put(y1.at[:, :, xx], rx2.at[n], rx2_s.at[n], rx2_r.at[n], dev(x=xx))
    for yy in y_peers:
        arrived(ty.at[yy], t_s.at[0], t_r.at[5 + yy])
    summed = ty[0]
    for n in range(1, NY):
        summed = summed + ty[n]
    th[0] = summed
    put(th.at[0], th.at[1], t_s.at[11], t_r.at[13], h_peer)

    summed = x1[:, y]
    for yy in y_peers:
        arrived(ry2.at[yy], ry2_s.at[0], ry2_r.at[yy])
        summed = summed + ry2[yy]
    zz[2:4] = summed
    summed = y1[:, :, x]
    for n in range(3):
        arrived(rx2.at[n], rx2_s.at[n], rx2_r.at[n])
        summed = summed + rx2[n]
    zz[0:2] = summed
    put(zz.at[:, 1 - h], rh, h_s, h_r, h_peer)
    arrived(th.at[1], t_s.at[0], t_r.at[13])
    lagged = hankel((th[0] + th[1]) * (1.0 / math.sqrt(ms.shape[0] // 3 * domains)))
    arrived(rh, h_s, h_r)
    final = zz[:, h] + rh[...]
    flux = [final[0] * final[1 + b] for b in range(3)]

    here = (h * NM + m) * NC + c
    sz[here] = jnp.concatenate(
        [jnp.sum(flux[b], axis=0, keepdims=True) for b in range(3)] + [jnp.zeros((5, T), F32)], axis=0
    )
    for n, (hh, mm, cc) in enumerate(z_peers):
        put(sz.at[here], sz.at[here], sz_s.at[n], sz_r.at[here], dev(h=hh, m=mm, c=cc))
    for b in range(3):
        flux_out[0, :, b, :] = flux[b]
    corr_out[0] = correlate(flux, lagged)[:, :LAGS]
    for hh, mm, cc in z_peers:
        there = (hh * NM + mm) * NC + cc
        arrived(sz.at[there], sz_s.at[0], sz_r.at[there])
    summed = sz[0]
    for n in range(1, 16):
        summed = summed + sz[n]
    sy[y] = summed
    for k, yy in enumerate(y_peers):
        put(sy.at[y], sy.at[y], sy_s.at[k], sy_r.at[y], dev(y=yy))
    for yy in y_peers:
        arrived(sy.at[yy], sy_s.at[0], sy_r.at[yy])
    summed = sy[0]
    for n in range(1, NY):
        summed = summed + sy[n]
    sx[x] = summed
    for k, xx in enumerate(x_peers):
        put(sx.at[x], sx.at[x], sx_s.at[k], sx_r.at[x], dev(x=xx))
    for xx in x_peers:
        arrived(sx.at[xx], sx_s.at[0], sx_r.at[xx])
    slab = ((sx[0] + sx[1]) + sx[2]) + sx[3]
    slab = correlate([jnp.broadcast_to(slab[b : b + 1, :], (8, T)) for b in range(3)], lagged)
    slab_out[...] = slab[0:1, :LAGS] * (1.0 / math.sqrt(NM * domains * K))

    for copy in sends:
        copy.wait_send()
    for when, copy in ghost_sends():
        pl.when(when)(copy.wait_send)


def per_device(velocity, local_virial, ghost_virial, eigvec, ghost_slot, counts):
    rows, modes = eigvec.shape
    vmem = pltpu.VMEM
    dma = pltpu.SemaphoreType.DMA
    scratch = [
        vmem((rows, modes), BF16),
        vmem((rows, 4 * T), BF16),
        vmem((2 * FACE, 3 * T), BF16),
        vmem((1, T), jnp.int32),
        vmem((2, FACE, 3 * T), BF16),
        vmem((2, FACE, 3 * T), BF16),
        vmem((4, NY, NH, NX, NC, K, T), F32),
        vmem((4, NY, NH, NX, K, T), F32),
        vmem((4, NY, NH, NX, K, T), F32),
        vmem((NY, 2, NH, NX, K, T), F32),
        vmem((3, 2, NY, NH, K, T), F32),
        vmem((2, NY, NH, K, T), F32),
        vmem((NY, 2, NH, K, T), F32),
        vmem((2, NH, NX, K, T), F32),
        vmem((3, 2, NH, K, T), F32),
        vmem((4, NH, K, T), F32),
        vmem((4, K, T), F32),
        vmem((8, T), F32),
        vmem((8, T), F32),
        vmem((NX, 8, T), F32),
        vmem((NY, 8, T), F32),
        vmem((2, 8, T), F32),
        vmem((16, 8, T), F32),
        vmem((NY, 8, T), F32),
        vmem((NX, 8, T), F32),
        dma((12,)),
        dma((2, 2)), dma((2,)),
        dma((4,)), dma((4,)),
        dma((3, 4)), dma((3, 4)),
        dma((8,)), dma((8,)),
        dma((8,)), dma((8,)),
        dma((3,)), dma((3,)),
        dma, dma,
        dma((12,)), dma((14,)),
        dma((15,)), dma((16,)),
        dma((7,)), dma((8,)),
        dma((3,)), dma((4,)),
    ]
    anywhere = pl.BlockSpec(memory_space=pl.ANY)
    in_vmem = pl.BlockSpec(memory_space=vmem)
    flux, corr, slab = pl.pallas_call(
        kernel,
        out_shape=(
            jax.ShapeDtypeStruct((1, K, 3, T), F32),
            jax.ShapeDtypeStruct((1, K, LAGS), F32),
            jax.ShapeDtypeStruct((1, LAGS), F32),
        ),
        in_specs=[anywhere] * 5 + [pl.BlockSpec(memory_space=pltpu.SMEM)],
        out_specs=(in_vmem, in_vmem, in_vmem),
        scratch_shapes=scratch,
        compiler_params=pltpu.CompilerParams(
            collective_id=0, has_side_effects=True, vmem_limit_bytes=56 * 2**20
        ),
        name="green_kubo",
    )(velocity, local_virial, ghost_virial, eigvec, ghost_slot.reshape(1, T), counts)
    return flux, corr, slab.reshape(LAGS)


def solution(mesh):
    return jax.shard_map(
        per_device,
        mesh=mesh,
        in_specs=(
            P("atom", None),
            P("atom", None),
            P("atom", None),
            P("atom", "mode"),
            P("atom"),
            P("atom"),
        ),
        out_specs=(P("mode", "atom", None, None), P("mode", "atom", None), P()),
        check_vma=False,
    )
```

time: 1720 us -> 68.6 us (0.04)
  blocking collectives: 909 us -> 0 us
  waiting for transfers between devices: 722 us -> 0 us
  Pallas kernels: 0 us -> 63.3 us
  local copies, waits for them, and re-layouts: 44.6 us -> 3.76 us
    psum x2 -> x0, blocking collectives: 909 us -> none  [the longest x1 808 us: per_device(): lax.psum(current_part, 'atom') / math.sqrt(slot_rows // 3 * domains)]
    psum x1 -> x0, waiting for transfers between devices: 722 us -> none  [per_device(): summed = lax.psum(jnp.concatenate([speeds, loads], axis=1), 'atom')]
    pallas_call x0 -> x1, Pallas kernels: none -> 63.3 us  [per_device(): pl.pallas_call(kernel, out_shape=(jax.ShapeDtypeStruct((1, K, 3, T), F32)...]
    gather x2 -> x0, local copies, waits for them, and re-layouts: 31.6 us -> none  [per_device(): hankel = padded[:, lag_index]]
  transfers between devices with their start and end apart: 3 -> 0, of which waited for: 1 -> 0; matrix products, arithmetic and copies ran while one was open for 3% -> 0% of each run, Pallas kernels for 0% -> 0%
where the time goes in v1:
time: 68.6 us; the launch traced here: 68.3 us
  Pallas kernels  63.3 us (92%)
  local copies, waits for them, and re-layouts  3.76 us (5%)
  between operations  1.29 us (2%)
    pallas_call x1, Pallas kernels, per_device(): pl.pallas_call(kernel, out_shape=(jax.ShapeDtypeStruct((1, K, 3, T), F32)...  63.3 us
    unnamed x3, local copies, waits for them, and re-layouts  3.76 us

profile of v1, /device:TPU:1, one launch (start us, length us, event | category | flops | bytes accessed | tf_op | source)
XLA Modules:
  0.0 68.3 jit_solution(1081288483134547795)
XLA Ops:
  1.3 63.3 %green_kubo.1 = (f32[1,8,3,128]{3,2,1,0:T(4,128)}, f32[1,8,64]{2,1,0:T(8,128)}, f32[1,64]{1,0:T(1,128)}) custom-call(bf16[1536,128]{1,0:T(8,128)(2,1)} %vel.1, bf16[1536,384]{1,0:T(8,128)(2,1)} %vir.1, bf16[384,384]{1,0:T(8,128)(2,1)} %gho.1, bf16[1536,1024]{1,0:T(8,128)(2,1)} %eig.1, s32[1,128]{1,0:T(1,128)} %bitcast.2, s32[1]{0:T(128)S(6)} %copy.12.counts), custom_call_target="tpu_custom_call" | custom-call | tf_op jit(solution)/shard_map/green_kubo/pallas_call | solution.py:349
  64.6 1.3 %copy.9 = f32[1,8,3,128]{3,1,2,0:T(8,128)} copy(f32[1,8,3,128]{3,2,1,0:T(4,128)} %get-tuple-element.9) | data formatting | bytes 24576
  65.9 1.3 %copy.13 = f32[1,8,64]{2,1,0:T(8,128)} copy(f32[1,8,64]{2,1,0:T(8,128)} %get-tuple-element.16) | data formatting | bytes 4096
  67.2 1.2 %copy.14 = f32[64]{0:T(128)} copy(f32[64]{0:T(128)} %bitcast.3) | data formatting | bytes 512

commit v2 on v0

v2 whole, which is shorter than its diff:
```python
import functools
import math

import jax
import jax.numpy as jnp
from jax import lax
from jax.experimental import pallas as pl
from jax.experimental.pallas import tpu as pltpu
from jax.sharding import PartitionSpec as P

MESH = pl.DeviceIdType.MESH
F32 = jnp.float32
BF16 = jnp.bfloat16
HIGHEST = lax.Precision.HIGHEST
NY, NH, NX, NC, NM = 8, 2, 4, 2, 4
T = 128
K = 8
FACE = 192
LAGS = 64


def dot_rows(left, right):
    return lax.dot_general(left, right, (((0,), (0,)), ((), ())), preferred_element_type=F32)


def iota(shape, dim):
    return lax.broadcasted_iota(jnp.int32, shape, dim)


def placing(slots, side):
    first = 64 * (1 - side)
    lowest = 64 * side
    ghost = iota((T, FACE), 0) - first
    third = lax.shift_right_logical(iota((T, FACE), 1) * 171, 9)
    spread = jnp.where(ghost == third, 1.0, 0.0).astype(BF16)
    slot = (slots - lowest).astype(F32).astype(BF16)
    slot = jnp.dot(jnp.broadcast_to(slot, (8, T)), spread, preferred_element_type=F32)
    lane = iota((8, FACE), 1)
    third = lax.shift_right_logical(lane * 171, 9)
    target = 3 * slot.astype(jnp.int32) + (lane - 3 * third)
    return jnp.where(iota((FACE, FACE), 0) == target[0:1, :], 1.0, 0.0).astype(BF16)


def hankel(total):
    parts = []
    for b in range(3):
        row = jnp.concatenate([total[:, b * T : (b + 1) * T], jnp.zeros((1, T), F32)], axis=1)
        row = jnp.broadcast_to(row, (T, 2 * T))
        parts.append(pltpu.roll(row, T + 1, 1, stride=1, stride_axis=0)[:, :T])
    flipped = jnp.concatenate(parts, axis=1)
    flip = jnp.where(iota((T, T), 0) + iota((T, T), 1) == T - 1, 1.0, 0.0).astype(F32)
    return jnp.dot(flip, flipped, precision=HIGHEST, preferred_element_type=F32)


def correlate(parts, lagged):
    out = None
    for b in range(3):
        term = jnp.dot(
            parts[b], lagged[:, b * T : (b + 1) * T], precision=HIGHEST, preferred_element_type=F32
        )
        out = term if out is None else out + term
    return out / (T - iota(out.shape, 1)).astype(F32)


def kernel(
    vel, vir, gho, eig, slots, counts, out,
    ev, ms, nv, rs, gh, ep, vp, part, cr, cs,
    rx, x1, ry, rr, rh, ryb, y1b, rxb, rhc, h1c, rxc, x1c, ryc,
    tp, tc, tx, ty, th, sz, sp,
    load_sem, gh_s, gh_r, rs_s, rs_r, c0_s, c0_r, c_s, c_r, rx_s, rx_r, ry_s, ry_r, rh_s, rh_r,
    ryb_s, ryb_r, rxb_s, rxb_r, rhc_s, rhc_r, rxc_s, rxc_r, ryc_s, ryc_r,
    t_s, t_r, sz_s, sz_r, sp_s, sp_r, hello,
):
    a = lax.axis_index("atom")
    m = lax.axis_index("mode")
    c, x, h, y = lax.rem(a, 2), lax.rem(lax.div(a, 2), 4), lax.rem(lax.div(a, 8), 2), lax.div(a, 16)
    place = lax.rem(a, 8)

    def dev(y=y, h=h, x=x, c=c, m=m):
        return (((y * NH + h) * NX + x) * NC + c, m)

    core = dev(c=1 - c)
    h_peer = dev(h=1 - h)
    x_peers = [lax.rem(x + k, NX) for k in range(1, NX)]
    y_peers = [lax.rem(y + k, NY) for k in range(1, NY)]
    z_peers = [
        (lax.rem(h + i // 8, NH), lax.rem(m + (i // 2) % 4, NM), lax.rem(c + i % 2, NC))
        for i in range(1, 16)
    ]
    p_peers = [(lax.rem(y + i // 4, NY), lax.rem(x + i % 4, NX)) for i in range(1, 32)]
    domains = NY * NH * NX * NC
    above = (lax.rem(a + 1, domains), jnp.where(place == 7, 3 - m, m))
    below = (lax.rem(a + domains - 1, domains), jnp.where(place == 0, 3 - m, m))

    barrier = pltpu.get_barrier_semaphore()
    greeted = [above, below, h_peer] + [dev(y=lax.rem(y + k, NY)) for k in (4, 3, 5, 2, 6, 1, 7)]
    m_peers = [dev(m=lax.rem(m + k, NM)) for k in range(1, NM)]
    greeted += [dev(x=xx) for xx in x_peers] + m_peers
    for device in greeted:
        pl.semaphore_signal(barrier, 1, device_id=device, device_id_type=MESH)
    loads = [
        pltpu.make_async_copy(counts, nv, load_sem.at[0]),
        pltpu.make_async_copy(vel, ms.at[:, 0:T], load_sem.at[1]),
        pltpu.make_async_copy(vir, ms.at[:, T:], load_sem.at[2]),
    ]
    loads += [
        pltpu.make_async_copy(
            eig.at[pl.ds(192 * i, 192)], ev.at[pl.ds(192 * i, 192)], load_sem.at[3 + i]
        )
        for i in range(8)
    ]
    for load in loads:
        load.start()

    sends = []

    class Copy:
        def __init__(self, src, dst, send_sem, recv_sem, device, into=None, in_sem=None):
            self.there = pltpu.make_async_remote_copy(
                src_ref=src, dst_ref=dst, send_sem=send_sem, recv_sem=recv_sem,
                device_id=device, device_id_type=MESH,
            )
            self.there.start()
            into = dst if into is None else into
            in_sem = recv_sem if in_sem is None else in_sem
            self.back = pltpu.make_async_remote_copy(
                src_ref=into, dst_ref=into, send_sem=send_sem, recv_sem=in_sem,
                device_id=device, device_id_type=MESH,
            )
            sends.append(self.there)

        def arrive(self):
            self.back.wait_recv()

    def sent():
        for copy in sends:
            copy.wait_send()
        sends.clear()

    for load in loads[:3]:
        load.wait()
    alive = jnp.where(iota((ms.shape[0], T), 0) < 3 * nv[0], 1.0, 0.0).astype(BF16)
    for q in range(4):
        ms[:, q * T : (q + 1) * T] = ms[:, q * T : (q + 1) * T] * alive

    pl.semaphore_wait(barrier, len(greeted))
    places = [
        Copy(slots, rs.at[0], rs_s.at[0], rs_r.at[0], above),
        Copy(slots, rs.at[1], rs_s.at[1], rs_r.at[1], below),
    ]
    ghost_copies = []
    for b in range(3):
        cols = pl.ds(b * T, T)
        ghost_copies += [
            Copy(gho.at[pl.ds(FACE, FACE), cols], gh.at[b, 0], gh_s.at[b, 0], gh_r.at[b, 0], above),
            Copy(gho.at[pl.ds(0, FACE), cols], gh.at[b, 1], gh_s.at[b, 1], gh_r.at[b, 1], below),
        ]

    for load in loads[3:]:
        load.wait()
    order = [lax.rem(lax.div(y, 2) + k, 4) for k in (1, 2, 3, 0)]
    core_first = []
    for k, j in enumerate(order):
        cols = pl.ds(pl.multiple_of(j * 256, 256), 256)
        two = pl.ds(2 * j, 2)
        acc = dot_rows(ev[:, cols], ms[...])
        for q in range(4):
            part[q, two] = acc[:, q * T : (q + 1) * T].reshape(2, NH, NX, NC, K, T)
        core_first.append(
            Copy(part.at[0, two, :, :, 1 - c], cr.at[0, two], c0_s.at[k], c0_r.at[k], core)
        )

    def x_sends(b, i, k, two):
        return [
            Copy(cs.at[b, two, :, xx], rx.at[i, n, two], rx_s.at[i, n, k], rx_r.at[i, n, k], dev(x=xx))
            for n, xx in enumerate(x_peers)
        ]

    def targets(k, j):
        return [2 * j, 2 * j + 1] if k < 3 else [y + 1 - 2 * lax.rem(y, 2)]

    def y_sends(i, k, j, copies):
        two = pl.ds(2 * j, 2)
        for copy in copies:
            copy.arrive()
        own = cs[2 * i, two, :, x]
        x1[i, two] = (own + rx[i, 0, two]) + (rx[i, 1, two] + rx[i, 2, two])
        return [
            (yy, Copy(x1.at[i, yy], ry.at[i, y], ry_s.at[i, 2 * k + n], ry_r.at[i, y], dev(y=yy),
                      ry.at[i, yy], ry_r.at[i, yy]))
            for n, yy in enumerate(targets(k, j))
        ]

    def gather_y(own, slots_of, copies):
        for yy, copy in copies:
            copy.arrive()
            own = own + slots_of[yy]
        return own

    xs0 = []
    for k, j in enumerate(order):
        two = pl.ds(2 * j, 2)
        core_first[k].arrive()
        cs[0, two] = part[0, two, :, :, c] + cr[0, two]
        xs0.append(x_sends(0, 0, k, two))

    total = dot_rows(ms[:, :T], ms[:, T:])
    for side in range(2):
        places[side].arrive()
        rows = pl.ds(FACE * side, FACE)
        put = placing(rs[side], side)
        ep[rows, :] = dot_rows(put, ev[rows, :]).astype(BF16)
        vp[rows, :] = dot_rows(put, ms[rows, 0:T]).astype(BF16)

    core_rest = []
    ysb, xs2, hsc = [], [], []

    def add_ghosts(b):
        for side in range(2):
            ghost_copies[2 * (b - 1) + side].arrive()
        ghosts = gh[b - 1].reshape(2 * FACE, T)
        for k, j in enumerate(order):
            cols = pl.ds(pl.multiple_of(j * 256, 256), 256)
            two = pl.ds(2 * j, 2)
            now = dot_rows(ep[:, cols], ghosts).reshape(2, NH, NX, NC, K, T)
            part[b, two] = part[b, two] + now
            core_rest.append(
                Copy(part.at[b, two, :, :, 1 - c], cr.at[b, two], c_s.at[b - 1, k], c_r.at[b - 1, k], core)
            )

    def send_on(b):
        for k, j in enumerate(order):
            two = pl.ds(2 * j, 2)
            core_rest[4 * (b - 1) + k].arrive()
            cs[b, two] = part[b, two, :, :, c] + cr[b, two]
            if b == 1:
                for n, yy in enumerate(targets(k, j)):
                    ysb.append(
                        (yy, Copy(cs.at[1, yy], ryb.at[y], ryb_s.at[2 * k + n], ryb_r.at[y], dev(y=yy),
                                  ryb.at[yy], ryb_r.at[yy]))
                    )
            elif b == 2:
                xs2.append(x_sends(2, 1, k, two))
            else:
                hsc.append(Copy(cs.at[3, two, 1 - h], rhc.at[two], rhc_s.at[k], rhc_r.at[k], h_peer))

    add_ghosts(1)
    add_ghosts(2)
    send_on(1)
    add_ghosts(3)
    send_on(2)

    diagonal = iota((T, T), 0) == iota((T, T), 1)
    parts = []
    for b in range(3):
        now = total[:, b * T : (b + 1) * T] + dot_rows(vp[...], gh[b].reshape(2 * FACE, T))
        parts.append(jnp.sum(jnp.where(diagonal, now, 0.0), axis=0, keepdims=True))
    tp[...] = jnp.concatenate(parts, axis=1)
    tot_core = Copy(tp, tc, t_s.at[0], t_r.at[0], core)
    send_on(3)

    tot_core.arrive()
    tx[x] = tp[...] + tc[...]
    tot_x = [
        Copy(tx.at[x], tx.at[x], t_s.at[1 + k], t_r.at[1 + x], dev(x=xx), tx.at[xx], t_r.at[1 + xx])
        for k, xx in enumerate(x_peers)
    ]
    ys0 = []
    for k, j in enumerate(order):
        ys0 += y_sends(0, k, j, xs0[k])
    ys2, xsc = [], []
    for k, j in enumerate(order):
        ys2 += y_sends(1, k, j, xs2[k])
    for k, j in enumerate(order):
        two = pl.ds(2 * j, 2)
        hsc[k].arrive()
        h1c[two] = cs[3, two, h] + rhc[two]
        xsc.append(
            [
                Copy(h1c.at[two, xx], rxc.at[n, two], rxc_s.at[n, k], rxc_r.at[n, k], dev(x=xx))
                for n, xx in enumerate(x_peers)
            ]
        )
    for device in m_peers:
        pl.semaphore_signal(hello, 1, device_id=device, device_id_type=MESH)
    for copy in tot_x:
        copy.arrive()
    ty[y] = ((tx[0] + tx[1]) + tx[2]) + tx[3]
    tot_y = [
        Copy(ty.at[y], ty.at[y], t_s.at[4 + k], t_r.at[5 + y], dev(y=yy), ty.at[yy], t_r.at[5 + yy])
        for k, yy in enumerate(y_peers)
    ]
    y1b[...] = gather_y(cs[1, y], ryb, ysb)
    xsb = [
        Copy(y1b.at[:, xx], rxb.at[n], rxb_s.at[n], rxb_r.at[n], dev(x=xx))
        for n, xx in enumerate(x_peers)
    ]
    ysc = []
    for k, j in enumerate(order):
        two = pl.ds(2 * j, 2)
        for copy in xsc[k]:
            copy.arrive()
        x1c[two] = (h1c[two, x] + rxc[0, two]) + (rxc[1, two] + rxc[2, two])
        for n, yy in enumerate(targets(k, j)):
            ysc.append(
                (yy, Copy(x1c.at[yy], ryc.at[y], ryc_s.at[2 * k + n], ryc_r.at[y], dev(y=yy),
                          ryc.at[yy], ryc_r.at[yy]))
            )

    def h_send(b):
        return Copy(rr.at[b, 1 - h], rh.at[b], rh_s.at[b], rh_r.at[b], h_peer)

    rr[0] = gather_y(x1[0, y], ry.at[0], ys0)
    hs = [h_send(0)]
    for copy in tot_y:
        copy.arrive()
    summed = ty[0]
    for n in range(1, NY):
        summed = summed + ty[n]
    th[0] = summed
    tot_h = Copy(th.at[0], th.at[1], t_s.at[11], t_r.at[13], h_peer)
    rr[2] = gather_y(x1[1, y], ry.at[1], ys2)
    hs.append(h_send(2))
    summed = y1b[:, x]
    for n, copy in enumerate(xsb):
        copy.arrive()
        summed = summed + rxb[n]
    rr[1] = summed
    hs.insert(1, h_send(1))
    tot_h.arrive()
    lagged = hankel((th[0] + th[1]) * (1.0 / math.sqrt(ms.shape[0] // 3 * domains)))
    last = gather_y(x1c[y], ryc, ysc)
    final = []
    for b in range(3):
        hs[b].arrive()
        final.append(rr[b, h] + rh[b])
    final.append(last)
    flux = [final[0] * final[1 + b] for b in range(3)]

    here = (h * NM + m) * NC + c
    sz[here] = jnp.concatenate([jnp.sum(flux[b], axis=0, keepdims=True) for b in range(3)], axis=1)
    pl.semaphore_wait(hello, NM - 1)
    szs = []
    for n, (hh, mm, cc) in enumerate(z_peers):
        there = (hh * NM + mm) * NC + cc
        szs.append(
            Copy(sz.at[here], sz.at[here], sz_s.at[n], sz_r.at[here], dev(h=hh, m=mm, c=cc),
                 sz.at[there], sz_r.at[there])
        )
    for b in range(3):
        out[b] = flux[b]
    out[3] = correlate(flux, lagged)
    sent()
    for copy in szs:
        copy.arrive()
    summed = sz[0]
    for n in range(1, 16):
        summed = summed + sz[n]
    here = y * NX + x
    sp[here] = summed
    sps = []
    for n, (yy, xx) in enumerate(p_peers):
        there = yy * NX + xx
        sps.append(
            Copy(sp.at[here], sp.at[here], sp_s.at[n], sp_r.at[here], dev(y=yy, x=xx),
                 sp.at[there], sp_r.at[there])
        )
    for copy in sps:
        copy.arrive()
    slab = sp[0]
    for n in range(1, 32):
        slab = slab + sp[n]
    slab = correlate([jnp.broadcast_to(slab[:, b * T : (b + 1) * T], (8, T)) for b in range(3)], lagged)
    out[4] = slab * (1.0 / math.sqrt(NM * domains * K))
    sent()


def deliver(held, flux, corr, slab):
    flux[0] = held[0:3]
    corr[0] = held[3, :, :LAGS]
    slab[...] = held[4, 0:1, :LAGS]


def per_device(velocity, local_virial, ghost_virial, eigvec, ghost_slot, counts):
    rows, modes = eigvec.shape
    vmem = pltpu.VMEM
    dma = pltpu.SemaphoreType.DMA
    scratch = [
        vmem((rows, modes), BF16),
        vmem((rows, 4 * T), BF16),
        pltpu.SMEM((1,), jnp.int32),
        vmem((2, 1, T), jnp.int32),
        vmem((3, 2, FACE, T), BF16),
        vmem((2 * FACE, modes), BF16),
        vmem((2 * FACE, T), BF16),
        vmem((4, NY, NH, NX, NC, K, T), F32),
        vmem((4, NY, NH, NX, K, T), F32),
        vmem((4, NY, NH, NX, K, T), F32),
        vmem((2, 3, NY, NH, K, T), F32),
        vmem((2, NY, NH, K, T), F32),
        vmem((2, NY, NH, K, T), F32),
        vmem((3, NH, K, T), F32),
        vmem((3, K, T), F32),
        vmem((NY, NH, NX, K, T), F32),
        vmem((NH, NX, K, T), F32),
        vmem((3, NH, K, T), F32),
        vmem((NY, NX, K, T), F32),
        vmem((NY, NX, K, T), F32),
        vmem((3, NY, K, T), F32),
        vmem((NY, K, T), F32),
        vmem((NY, K, T), F32),
        vmem((1, 3 * T), F32),
        vmem((1, 3 * T), F32),
        vmem((NX, 1, 3 * T), F32),
        vmem((NY, 1, 3 * T), F32),
        vmem((2, 1, 3 * T), F32),
        vmem((16, 1, 3 * T), F32),
        vmem((32, 1, 3 * T), F32),
        dma((11,)),
        dma((3, 2)), dma((3, 2)),
        dma((2,)), dma((2,)),
        dma((4,)), dma((4,)),
        dma((3, 4)), dma((3, 4)),
        dma((2, 3, 4)), dma((2, 3, 4)),
        dma((2, 8)), dma((2, 8)),
        dma((3,)), dma((3,)),
        dma((8,)), dma((8,)),
        dma((3,)), dma((3,)),
        dma((4,)), dma((4,)),
        dma((3, 4)), dma((3, 4)),
        dma((8,)), dma((8,)),
        dma((12,)), dma((14,)),
        dma((15,)), dma((16,)),
        dma((31,)), dma((32,)),
        pltpu.SemaphoreType.REGULAR,
    ]
    held = pl.pallas_call(
        kernel,
        out_shape=jax.ShapeDtypeStruct((5, K, T), F32),
        in_specs=[pl.BlockSpec(memory_space=pl.ANY)] * 6,
        out_specs=pl.BlockSpec(memory_space=vmem),
        scratch_shapes=scratch,
        compiler_params=pltpu.CompilerParams(
            collective_id=0, has_side_effects=True, vmem_limit_bytes=56 * 2**20
        ),
        name="green_kubo",
    )(velocity, local_virial, ghost_virial, eigvec, ghost_slot.reshape(1, T), counts)
    flux, corr, slab = pl.pallas_call(
        deliver,
        out_shape=(
            jax.ShapeDtypeStruct((1, 3, K, T), F32),
            jax.ShapeDtypeStruct((1, K, LAGS), F32),
            jax.ShapeDtypeStruct((1, LAGS), F32),
        ),
        name="deliver",
    )(held)
    return jnp.transpose(flux, (0, 2, 1, 3)), corr, slab.reshape(LAGS)


def solution(mesh):
    return jax.shard_map(
        per_device,
        mesh=mesh,
        in_specs=(
            P("atom", None),
            P("atom", None),
            P("atom", None),
            P("atom", "mode"),
            P("atom"),
            P("atom"),
        ),
        out_specs=(P("mode", "atom", None, None), P("mode", "atom", None), P()),
        check_vma=False,
    )
```

time: 1720 us -> 60.3 us (0.04)
  blocking collectives: 909 us -> 0 us
  waiting for transfers between devices: 722 us -> 0 us
  Pallas kernels: 0 us -> 58.9 us
  local copies, waits for them, and re-layouts: 44.6 us -> 0 us
    psum x2 -> x0, blocking collectives: 909 us -> none  [the longest x1 808 us: per_device(): lax.psum(current_part, 'atom') / math.sqrt(slot_rows // 3 * domains)]
    psum x1 -> x0, waiting for transfers between devices: 722 us -> none  [per_device(): summed = lax.psum(jnp.concatenate([speeds, loads], axis=1), 'atom')]
    pallas_call x0 -> x2, Pallas kernels: none -> 58.9 us  [the longest x1 57.5 us: per_device(): pl.pallas_call(kernel, out_shape=jax.ShapeDtypeStruct((5, K, T), F32), in...]
    gather x2 -> x0, local copies, waits for them, and re-layouts: 31.6 us -> none  [per_device(): hankel = padded[:, lag_index]]
  transfers between devices with their start and end apart: 3 -> 0, of which waited for: 1 -> 0; matrix products, arithmetic and copies ran while one was open for 3% -> 0% of each run, Pallas kernels for 0% -> 0%
where the time goes in v2:
time: 60.3 us; the launch traced here: 60.1 us
  Pallas kernels  58.9 us (98%)
  between operations  1.29 us (2%)
    pallas_call x1, Pallas kernels, per_device(): pl.pallas_call(kernel, out_shape=jax.ShapeDtypeStruct((5, K, T), F32), in...  57.5 us
    pallas_call x1, Pallas kernels, per_device(): pl.pallas_call(deliver, out_shape=(jax.ShapeDtypeStruct((1, 3, K, T), F32...  1.34 us

profile of v2, /device:TPU:1, one launch (start us, length us, event | category | flops | bytes accessed | tf_op | source)
XLA Modules:
  0.0 60.1 jit_solution(16581697707640379029)
XLA Ops:
  1.3 57.5 %green_kubo.1.held = f32[5,8,128]{2,1,0:T(8,128)} custom-call(bf16[1536,128]{1,0:T(8,128)(2,1)} %vel.1, bf16[1536,384]{1,0:T(8,128)(2,1)} %vir.1, bf16[384,384]{1,0:T(8,128)(2,1)} %gho.1, bf16[1536,1024]{1,0:T(8,128)(2,1)} %eig.1, s32[1,128]{1,0:T(1,128)} %bitcast.3, s32[1]{0:T(128)S(6)} %copy.9.counts), custom_call_target="tpu_custom_call" | custom-call | tf_op jit(solution)/shard_map/green_kubo/pallas_call | solution.py:437
  58.8 1.3 %deliver.1 = (f32[1,3,8,128]{3,2,1,0:T(8,128)}, f32[1,8,64]{2,1,0:T(8,128)}, f32[1,64]{1,0:T(1,128)}) custom-call(f32[5,8,128]{2,1,0:T(8,128)} %green_kubo.1.held), custom_call_target="tpu_custom_call" | custom-call | tf_op jit(solution)/shard_map/deliver/pallas_call | solution.py:448

commit v3 on v0

v3 whole, which is shorter than its diff:
```python
import functools
import math

import jax
import jax.numpy as jnp
from jax import lax
from jax.experimental import pallas as pl
from jax.experimental.pallas import tpu as pltpu
from jax.sharding import PartitionSpec as P

MESH = pl.DeviceIdType.MESH
F32 = jnp.float32
BF16 = jnp.bfloat16
HIGHEST = lax.Precision.HIGHEST
NY, NH, NX, NC, NM = 8, 2, 4, 2, 4
T = 128
K = 8
FACE = 192
LAGS = 64


def dot_rows(left, right):
    return lax.dot_general(left, right, (((0,), (0,)), ((), ())), preferred_element_type=F32)


def iota(shape, dim):
    return lax.broadcasted_iota(jnp.int32, shape, dim)


def placing(slots, side):
    first = 64 * (1 - side)
    lowest = 64 * side
    ghost = iota((T, FACE), 0) - first
    third = lax.shift_right_logical(iota((T, FACE), 1) * 171, 9)
    spread = jnp.where(ghost == third, 1.0, 0.0).astype(BF16)
    slot = (slots - lowest).astype(F32).astype(BF16)
    slot = jnp.dot(jnp.broadcast_to(slot, (8, T)), spread, preferred_element_type=F32)
    lane = iota((8, FACE), 1)
    third = lax.shift_right_logical(lane * 171, 9)
    target = 3 * slot.astype(jnp.int32) + (lane - 3 * third)
    return jnp.where(iota((FACE, FACE), 0) == target[0:1, :], 1.0, 0.0).astype(BF16)


def hankel(total):
    parts = []
    for b in range(3):
        row = jnp.concatenate([total[:, b * T : (b + 1) * T], jnp.zeros((1, T), F32)], axis=1)
        row = jnp.broadcast_to(row, (T, 2 * T))
        parts.append(pltpu.roll(row, T + 1, 1, stride=1, stride_axis=0)[:, :T])
    flipped = jnp.concatenate(parts, axis=1)
    flip = jnp.where(iota((T, T), 0) + iota((T, T), 1) == T - 1, 1.0, 0.0).astype(F32)
    lagged = jnp.dot(flip, flipped, precision=HIGHEST, preferred_element_type=F32)
    return jnp.concatenate([lagged[:, b * T : (b + 1) * T] for b in range(3)], axis=0)


def correlate(flux, lagged):
    out = jnp.dot(flux, lagged, precision=HIGHEST, preferred_element_type=F32)
    return out / (T - iota(out.shape, 1)).astype(F32)


class Group:
    def __init__(self, sems, index):
        self.send_sem, self.recv_sem = sems.at[0, index], sems.at[1, index]

    def describe(self, src, dst, device):
        return pltpu.make_async_remote_copy(
            src_ref=src, dst_ref=dst, send_sem=self.send_sem, recv_sem=self.recv_sem,
            device_id=device, device_id_type=MESH,
        )

    def put(self, src, dst, device):
        self.device = device
        self.describe(src, dst, device).start()

    def arrive(self, whole):
        self.whole = whole
        self.describe(whole, whole, self.device).wait_recv()

    def left(self):
        self.describe(self.whole, self.whole, self.device).wait_send()


def kernel(
    vel, vir, gho, eig, slots, counts, out,
    ev, ms, nv, rs, gh, ep, vp, part, cr, cs,
    rx, x1, ry, rr, rh, ryb, y1b, rxb, rhc, h1c, rxc, x1c, ryc,
    tp, tc, tx, ty, th, sz, sp,
    load_sem, sems, relay,
):
    a = lax.axis_index("atom")
    m = lax.axis_index("mode")
    c, x, h, y = lax.rem(a, 2), lax.rem(lax.div(a, 2), 4), lax.rem(lax.div(a, 8), 2), lax.div(a, 16)
    z = h * NM + m
    place = lax.rem(a, 8)

    def dev(y=y, h=h, x=x, c=c, m=m):
        return (((y * NH + h) * NX + x) * NC + c, m)

    core = dev(c=1 - c)
    h_peer = dev(h=1 - h)
    x_peers = [lax.rem(x + k, NX) for k in range(1, NX)]
    y_peers = [lax.rem(y + k, NY) for k in range(1, NY)]
    z_peers = [(lax.rem(z + i // 2, 8), lax.rem(c + i % 2, NC)) for i in range(1, 16)]
    p_peers = [(lax.rem(y + i // 4, NY), lax.rem(x + i % 4, NX)) for i in range(1, 32)]
    domains = NY * NH * NX * NC
    above = (lax.rem(a + 1, domains), jnp.where(place == 7, 3 - m, m))
    below = (lax.rem(a + domains - 1, domains), jnp.where(place == 0, 3 - m, m))
    near = [dev(x=x_peers[0]), dev(x=x_peers[2]), dev(y=y_peers[0]), dev(y=y_peers[6])]
    near += [dev(h=lax.div(zz, NM), m=lax.rem(zz, NM)) for zz in (lax.rem(z + 1, 8), lax.rem(z + 7, 8))]

    barrier = pltpu.get_barrier_semaphore()
    for device in [above, below] + near:
        pl.semaphore_signal(barrier, 1, device_id=device, device_id_type=MESH)
    loads = [
        pltpu.make_async_copy(counts, nv, load_sem.at[0]),
        pltpu.make_async_copy(vel, ms.at[:, 0:T], load_sem.at[1]),
        pltpu.make_async_copy(vir, ms.at[:, T:], load_sem.at[2]),
    ]
    loads += [
        pltpu.make_async_copy(eig.at[pl.ds(384 * i, 384)], ev.at[pl.ds(384 * i, 384)], load_sem.at[3 + i])
        for i in range(4)
    ]
    for load in loads:
        load.start()

    used = [0]

    def group():
        used[0] += 1
        return Group(sems, used[0] - 1)

    def tell(step):
        for device in near:
            pl.semaphore_signal(relay.at[step], 1, device_id=device, device_id_type=MESH)

    def told(step):
        pl.semaphore_wait(relay.at[step], len(near))

    pl.semaphore_wait(barrier, 2 + len(near))
    places = [group(), group()]
    places[0].put(slots, rs.at[0], above)
    places[1].put(slots, rs.at[1], below)
    ghost_copies = []
    for b in range(3):
        cols = pl.ds(b * T, T)
        for side, device in enumerate((above, below)):
            ghost_copies.append(group())
            ghost_copies[-1].put(gho.at[pl.ds(FACE * (1 - side), FACE), cols], gh.at[b, side], device)
    tell(0)

    for load in loads[:3]:
        load.wait()
    alive = jnp.where(iota((ms.shape[0], T), 0) < 3 * nv[0], 1.0, 0.0).astype(BF16)
    for q in range(4):
        ms[:, q * T : (q + 1) * T] = ms[:, q * T : (q + 1) * T] * alive

    for load in loads[3:]:
        load.wait()
    for j in range(4):
        acc = dot_rows(ev[:, 256 * j : 256 * (j + 1)], ms[...])
        for q in range(4):
            part[q, 2 * j : 2 * j + 2] = acc[:, q * T : (q + 1) * T].reshape(2, NH, NX, NC, K, T)
        if j == 1:
            told(0)
            tell(1)

    cores = []

    def core_send(b):
        cores.append(group())
        cores[-1].put(part.at[b, :, :, :, 1 - c], cr.at[b], core)

    def core_sum(b):
        cores[b].arrive(cr.at[b])
        cs[b] = part[b, :, :, :, c] + cr[b]

    def over_x(src, dst, cut):
        copies = group()
        for n, xx in enumerate(x_peers):
            copies.put(cut(src, xx), dst.at[n], dev(x=xx))
        return copies

    def over_y(src, dst):
        copies = group()
        for n, yy in enumerate(y_peers):
            copies.put(src.at[yy], dst.at[n], dev(y=yy))
        return copies

    def over_h(src, dst):
        copies = group()
        copies.put(src, dst, h_peer)
        return copies

    def gather(copies, own, slots_of):
        copies.arrive(slots_of)
        for n in range(slots_of.shape[0]):
            own = own + slots_of[n]
        return own

    core_send(0)
    told(1)
    tell(2)

    total = dot_rows(ms[:, :T], ms[:, T:])
    for side in range(2):
        places[side].arrive(rs.at[side])
        rows = pl.ds(FACE * side, FACE)
        put = placing(rs[side], side)
        ep[rows, :] = dot_rows(put, ev[rows, :]).astype(BF16)
        vp[rows, :] = dot_rows(put, ms[rows, 0:T]).astype(BF16)
    core_sum(0)
    xs0 = over_x(cs.at[0], rx.at[0], lambda ref, xx: ref.at[:, :, xx])
    told(2)

    def add_ghosts(b):
        for side in range(2):
            ghost_copies[2 * (b - 1) + side].arrive(gh.at[b - 1, side])
        ghosts = gh[b - 1].reshape(2 * FACE, T)
        for j in range(4):
            now = dot_rows(ep[:, 256 * j : 256 * (j + 1)], ghosts).reshape(2, NH, NX, NC, K, T)
            part[b, 2 * j : 2 * j + 2] = part[b, 2 * j : 2 * j + 2] + now
        core_send(b)

    add_ghosts(1)
    add_ghosts(2)
    core_sum(1)
    ysb = over_y(cs.at[1], ryb)
    add_ghosts(3)
    core_sum(2)
    xs2 = over_x(cs.at[2], rx.at[1], lambda ref, xx: ref.at[:, :, xx])

    diagonal = iota((T, T), 0) == iota((T, T), 1)
    parts = []
    for b in range(3):
        now = total[:, b * T : (b + 1) * T] + dot_rows(vp[...], gh[b].reshape(2 * FACE, T))
        parts.append(jnp.sum(jnp.where(diagonal, now, 0.0), axis=0, keepdims=True))
    core_sum(3)
    hsc = over_h(cs.at[3, :, 1 - h], rhc)
    tp[...] = jnp.concatenate(parts, axis=1)
    tot_core = group()
    tot_core.put(tp, tc, core)

    x1[0] = gather(xs0, cs[0, :, :, x], rx.at[0])
    ys0 = over_y(x1.at[0], ry.at[0])
    tot_core.arrive(tc)
    tx[x] = tp[...] + tc[...]
    tot_x = group()
    for xx in x_peers:
        tot_x.put(tx.at[x], tx.at[x], dev(x=xx))
    x1[1] = gather(xs2, cs[2, :, :, x], rx.at[1])
    ys2 = over_y(x1.at[1], ry.at[1])
    hsc.arrive(rhc)
    h1c[...] = cs[3, :, h] + rhc[...]
    xsc = over_x(h1c, rxc, lambda ref, xx: ref.at[:, xx])
    tot_x.arrive(tx.at[pl.ds(0, 3)])
    ty[y] = ((tx[0] + tx[1]) + tx[2]) + tx[3]
    tot_y = group()
    for yy in y_peers:
        tot_y.put(ty.at[y], ty.at[y], dev(y=yy))
    y1b[...] = gather(ysb, cs[1, y], ryb)
    xsb = over_x(y1b, rxb, lambda ref, xx: ref.at[:, xx])
    x1c[...] = gather(xsc, h1c[:, x], rxc)
    ysc = over_y(x1c, ryc)
    rr[0] = gather(ys0, x1[0, y], ry.at[0])
    hs0 = over_h(rr.at[0, 1 - h], rh.at[0])
    tot_y.arrive(ty.at[pl.ds(0, 7)])
    summed = ty[0]
    for n in range(1, NY):
        summed = summed + ty[n]
    th[0] = summed
    tot_h = over_h(th.at[0], th.at[1])
    rr[2] = gather(ys2, x1[1, y], ry.at[1])
    hs2 = over_h(rr.at[2, 1 - h], rh.at[2])
    rr[1] = gather(xsb, y1b[:, x], rxb)
    hs1 = over_h(rr.at[1, 1 - h], rh.at[1])
    tot_h.arrive(th.at[1])
    lagged = hankel((th[0] + th[1]) * (1.0 / math.sqrt(ms.shape[0] // 3 * domains)))
    last = gather(ysc, x1c[y], ryc)
    hs0.arrive(rh.at[0])
    hs2.arrive(rh.at[2])
    hs1.arrive(rh.at[1])
    final = [rr[b, h] + rh[b] for b in range(3)] + [last]
    flux = jnp.concatenate([final[0] * final[1 + b] for b in range(3)], axis=1)

    here = z * NC + c
    sz[here] = jnp.sum(flux, axis=0, keepdims=True)
    szs = group()
    for zz, cc in z_peers:
        szs.put(sz.at[here], sz.at[here], dev(h=lax.div(zz, NM), m=lax.rem(zz, NM), c=cc))
    for b in range(3):
        out[b] = flux[:, b * T : (b + 1) * T]
    out[3] = correlate(flux, lagged)
    for copies in places + ghost_copies + cores:
        copies.left()
    for copies in (xs0, ys0, hs0, ysb, xsb, hs1, xs2, ys2, hs2, hsc, xsc, ysc):
        copies.left()
    for copies in (tot_core, tot_x, tot_y, tot_h):
        copies.left()
    szs.arrive(sz.at[pl.ds(0, 15)])
    summed = sz[0]
    for n in range(1, 16):
        summed = summed + sz[n]
    there = y * NX + x
    sp[there] = summed
    sps = group()
    for yy, xx in p_peers:
        sps.put(sp.at[there], sp.at[there], dev(y=yy, x=xx))
    szs.left()
    sps.arrive(sp.at[pl.ds(0, 31)])
    slab = sp[0]
    for n in range(1, 32):
        slab = slab + sp[n]
    out[4] = correlate(jnp.broadcast_to(slab, (8, 3 * T)), lagged) * (1.0 / math.sqrt(NM * domains * K))
    sps.left()


def deliver(held, flux, corr, slab):
    flux[0] = held[0:3]
    corr[0] = held[3, :, :LAGS]
    slab[...] = held[4, 0:1, :LAGS]


def per_device(velocity, local_virial, ghost_virial, eigvec, ghost_slot, counts):
    rows, modes = eigvec.shape
    vmem = pltpu.VMEM
    dma = pltpu.SemaphoreType.DMA
    scratch = [
        vmem((rows, modes), BF16),
        vmem((rows, 4 * T), BF16),
        pltpu.SMEM((1,), jnp.int32),
        vmem((2, 1, T), jnp.int32),
        vmem((3, 2, FACE, T), BF16),
        vmem((2 * FACE, modes), BF16),
        vmem((2 * FACE, T), BF16),
        vmem((4, NY, NH, NX, NC, K, T), F32),
        vmem((4, NY, NH, NX, K, T), F32),
        vmem((4, NY, NH, NX, K, T), F32),
        vmem((2, 3, NY, NH, K, T), F32),
        vmem((2, NY, NH, K, T), F32),
        vmem((2, NY - 1, NH, K, T), F32),
        vmem((3, NH, K, T), F32),
        vmem((3, K, T), F32),
        vmem((NY - 1, NH, NX, K, T), F32),
        vmem((NH, NX, K, T), F32),
        vmem((3, NH, K, T), F32),
        vmem((NY, NX, K, T), F32),
        vmem((NY, NX, K, T), F32),
        vmem((3, NY, K, T), F32),
        vmem((NY, K, T), F32),
        vmem((NY - 1, K, T), F32),
        vmem((1, 3 * T), F32),
        vmem((1, 3 * T), F32),
        vmem((NX, 1, 3 * T), F32),
        vmem((NY, 1, 3 * T), F32),
        vmem((2, 1, 3 * T), F32),
        vmem((16, 1, 3 * T), F32),
        vmem((32, 1, 3 * T), F32),
        dma((7,)),
        dma((2, 32)),
        pltpu.SemaphoreType.REGULAR((3,)),
    ]
    held = pl.pallas_call(
        kernel,
        out_shape=jax.ShapeDtypeStruct((5, K, T), F32),
        in_specs=[pl.BlockSpec(memory_space=pltpu.HBM)] * 6,
        out_specs=pl.BlockSpec(memory_space=vmem),
        scratch_shapes=scratch,
        compiler_params=pltpu.CompilerParams(
            collective_id=0, has_side_effects=True, vmem_limit_bytes=56 * 2**20
        ),
        name="green_kubo",
    )(velocity, local_virial, ghost_virial, eigvec, ghost_slot.reshape(1, T), counts)
    flux, corr, slab = pl.pallas_call(
        deliver,
        out_shape=(
            jax.ShapeDtypeStruct((1, 3, K, T), F32),
            jax.ShapeDtypeStruct((1, K, LAGS), F32),
            jax.ShapeDtypeStruct((1, LAGS), F32),
        ),
        name="deliver",
    )(held)
    return jnp.transpose(flux, (0, 2, 1, 3)), corr, slab.reshape(LAGS)


def solution(mesh):
    return jax.shard_map(
        per_device,
        mesh=mesh,
        in_specs=(
            P("atom", None),
            P("atom", None),
            P("atom", None),
            P("atom", "mode"),
            P("atom"),
            P("atom"),
        ),
        out_specs=(P("mode", "atom", None, None), P("mode", "atom", None), P()),
        check_vma=False,
    )
```

time: 1720 us -> 57.6 us (0.03)
  blocking collectives: 909 us -> 0 us
  waiting for transfers between devices: 722 us -> 0 us
  Pallas kernels: 0 us -> 56.1 us
  local copies, waits for them, and re-layouts: 44.6 us -> 0 us
    psum x2 -> x0, blocking collectives: 909 us -> none  [the longest x1 808 us: per_device(): lax.psum(current_part, 'atom') / math.sqrt(slot_rows // 3 * domains)]
    psum x1 -> x0, waiting for transfers between devices: 722 us -> none  [per_device(): summed = lax.psum(jnp.concatenate([speeds, loads], axis=1), 'atom')]
    pallas_call x0 -> x2, Pallas kernels: none -> 56.1 us  [the longest x1 54.8 us: per_device(): pl.pallas_call(kernel, out_shape=jax.ShapeDtypeStruct((5, K, T), F32), in...]
    gather x2 -> x0, local copies, waits for them, and re-layouts: 31.6 us -> none  [per_device(): hankel = padded[:, lag_index]]
  transfers between devices with their start and end apart: 3 -> 0, of which waited for: 1 -> 0; matrix products, arithmetic and copies ran while one was open for 3% -> 0% of each run, Pallas kernels for 0% -> 0%
where the time goes in v3:
time: 57.6 us; the launch traced here: 57.4 us
  Pallas kernels  56.1 us (97%)
  between operations  1.29 us (2%)
    pallas_call x1, Pallas kernels, per_device(): pl.pallas_call(kernel, out_shape=jax.ShapeDtypeStruct((5, K, T), F32), in...  54.8 us
    pallas_call x1, Pallas kernels, per_device(): pl.pallas_call(deliver, out_shape=(jax.ShapeDtypeStruct((1, 3, K, T), F32...  1.34 us

profile of v3, /device:TPU:1, one launch (start us, length us, event | category | flops | bytes accessed | tf_op | source)
XLA Modules:
  0.0 57.4 jit_solution(5997660033542328917)
XLA Ops:
  1.3 54.8 %green_kubo.1.held = f32[5,8,128]{2,1,0:T(8,128)} custom-call(bf16[1536,128]{1,0:T(8,128)(2,1)} %vel.1, bf16[1536,384]{1,0:T(8,128)(2,1)} %vir.1, bf16[384,384]{1,0:T(8,128)(2,1)} %gho.1, bf16[1536,1024]{1,0:T(8,128)(2,1)} %eig.1, s32[1,128]{1,0:T(1,128)} %bitcast.3, s32[1]{0:T(128)S(6)} %copy.9.counts), custom_call_target="tpu_custom_call" | custom-call | tf_op jit(solution)/shard_map/green_kubo/pallas_call | solution.py:362
  56.0 1.3 %deliver.1 = (f32[1,3,8,128]{3,2,1,0:T(8,128)}, f32[1,8,64]{2,1,0:T(8,128)}, f32[1,64]{1,0:T(1,128)}) custom-call(f32[5,8,128]{2,1,0:T(8,128)} %green_kubo.1.held), custom_call_target="tpu_custom_call" | custom-call | tf_op jit(solution)/shard_map/deliver/pallas_call | solution.py:373

commit v4 on v3

--- a/solution.py
+++ b/solution.py
@@ -17,6 +17,7 @@
 K = 8
 FACE = 192
 LAGS = 64
+RING = (4, 3, 5, 2, 6, 1, 7)
 
 
 def dot_rows(left, right):
@@ -98,14 +99,15 @@
 
     core = dev(c=1 - c)
     h_peer = dev(h=1 - h)
-    x_peers = [lax.rem(x + k, NX) for k in range(1, NX)]
-    y_peers = [lax.rem(y + k, NY) for k in range(1, NY)]
-    z_peers = [(lax.rem(z + i // 2, 8), lax.rem(c + i % 2, NC)) for i in range(1, 16)]
-    p_peers = [(lax.rem(y + i // 4, NY), lax.rem(x + i % 4, NX)) for i in range(1, 32)]
+    x_peers = [lax.rem(x + k, NX) for k in (2, 1, 3)]
+    y_peers = [lax.rem(y + k, NY) for k in RING]
+    z_peers = [(lax.rem(z + k, 8), lax.rem(c + i, NC)) for k in RING for i in (1, 0)] + [(z, 1 - c)]
+    steps = sorted(range(1, 32), key=lambda i: -min(i // 4, NY - i // 4) - min(i % 4, NX - i % 4))
+    p_peers = [(lax.rem(y + i // 4, NY), lax.rem(x + i % 4, NX)) for i in steps]
     domains = NY * NH * NX * NC
     above = (lax.rem(a + 1, domains), jnp.where(place == 7, 3 - m, m))
     below = (lax.rem(a + domains - 1, domains), jnp.where(place == 0, 3 - m, m))
-    near = [dev(x=x_peers[0]), dev(x=x_peers[2]), dev(y=y_peers[0]), dev(y=y_peers[6])]
+    near = [dev(x=lax.rem(x + k, NX)) for k in (1, 3)] + [dev(y=lax.rem(y + k, NY)) for k in (1, 7)]
     near += [dev(h=lax.div(zz, NM), m=lax.rem(zz, NM)) for zz in (lax.rem(z + 1, 8), lax.rem(z + 7, 8))]
 
     barrier = pltpu.get_barrier_semaphore()
@@ -140,12 +142,12 @@
     places = [group(), group()]
     places[0].put(slots, rs.at[0], above)
     places[1].put(slots, rs.at[1], below)
-    ghost_copies = []
-    for b in range(3):
+    ghost_copies = {}
+    for b in (2, 0, 1):
         cols = pl.ds(b * T, T)
         for side, device in enumerate((above, below)):
-            ghost_copies.append(group())
-            ghost_copies[-1].put(gho.at[pl.ds(FACE * (1 - side), FACE), cols], gh.at[b, side], device)
+            ghost_copies[b, side] = group()
+            ghost_copies[b, side].put(gho.at[pl.ds(FACE * (1 - side), FACE), cols], gh.at[b, side], device)
     tell(0)
 
     for load in loads[:3]:
@@ -164,11 +166,11 @@
             told(0)
             tell(1)
 
-    cores = []
+    cores = {}
 
     def core_send(b):
-        cores.append(group())
-        cores[-1].put(part.at[b, :, :, :, 1 - c], cr.at[b], core)
+        cores[b] = group()
+        cores[b].put(part.at[b, :, :, :, 1 - c], cr.at[b], core)
 
     def core_sum(b):
         cores[b].arrive(cr.at[b])
@@ -201,7 +203,6 @@
     told(1)
     tell(2)
 
-    total = dot_rows(ms[:, :T], ms[:, T:])
     for side in range(2):
         places[side].arrive(rs.at[side])
         rows = pl.ds(FACE * side, FACE)
@@ -214,28 +215,29 @@
 
     def add_ghosts(b):
         for side in range(2):
-            ghost_copies[2 * (b - 1) + side].arrive(gh.at[b - 1, side])
+            ghost_copies[b - 1, side].arrive(gh.at[b - 1, side])
         ghosts = gh[b - 1].reshape(2 * FACE, T)
         for j in range(4):
             now = dot_rows(ep[:, 256 * j : 256 * (j + 1)], ghosts).reshape(2, NH, NX, NC, K, T)
             part[b, 2 * j : 2 * j + 2] = part[b, 2 * j : 2 * j + 2] + now
         core_send(b)
 
+    add_ghosts(3)
     add_ghosts(1)
+    core_sum(3)
+    hsc = over_h(cs.at[3, :, 1 - h], rhc)
     add_ghosts(2)
     core_sum(1)
     ysb = over_y(cs.at[1], ryb)
-    add_ghosts(3)
     core_sum(2)
     xs2 = over_x(cs.at[2], rx.at[1], lambda ref, xx: ref.at[:, :, xx])
 
+    total = dot_rows(ms[:, :T], ms[:, T:])
     diagonal = iota((T, T), 0) == iota((T, T), 1)
     parts = []
     for b in range(3):
         now = total[:, b * T : (b + 1) * T] + dot_rows(vp[...], gh[b].reshape(2 * FACE, T))
         parts.append(jnp.sum(jnp.where(diagonal, now, 0.0), axis=0, keepdims=True))
-    core_sum(3)
-    hsc = over_h(cs.at[3, :, 1 - h], rhc)
     tp[...] = jnp.concatenate(parts, axis=1)
     tot_core = group()
     tot_core.put(tp, tc, core)
@@ -247,11 +249,11 @@
     tot_x = group()
     for xx in x_peers:
         tot_x.put(tx.at[x], tx.at[x], dev(x=xx))
-    x1[1] = gather(xs2, cs[2, :, :, x], rx.at[1])
-    ys2 = over_y(x1.at[1], ry.at[1])
     hsc.arrive(rhc)
     h1c[...] = cs[3, :, h] + rhc[...]
     xsc = over_x(h1c, rxc, lambda ref, xx: ref.at[:, xx])
+    x1[1] = gather(xs2, cs[2, :, :, x], rx.at[1])
+    ys2 = over_y(x1.at[1], ry.at[1])
     tot_x.arrive(tx.at[pl.ds(0, 3)])
     ty[y] = ((tx[0] + tx[1]) + tx[2]) + tx[3]
     tot_y = group()
@@ -290,7 +292,7 @@
     for b in range(3):
         out[b] = flux[:, b * T : (b + 1) * T]
     out[3] = correlate(flux, lagged)
-    for copies in places + ghost_copies + cores:
+    for copies in places + list(ghost_copies.values()) + list(cores.values()):
         copies.left()
     for copies in (xs0, ys0, hs0, ysb, xsb, hs1, xs2, ys2, hs2, hsc, xsc, ysc):
         copies.left()

time: 57.6 us -> 55.4 us (0.962)
  Pallas kernels: 56.1 us -> 53.9 us
    pallas_call x1, Pallas kernels: 54.8 us -> 52.6 us  [per_device(): pl.pallas_call(kernel, out_shape=jax.ShapeDtypeStruct((5, K, T), F32), in...]
where the time goes in v4:
time: 55.4 us; the launch traced here: 55.2 us
  Pallas kernels  53.9 us (97%)
  between operations  1.29 us (2%)
    pallas_call x1, Pallas kernels, per_device(): pl.pallas_call(kernel, out_shape=jax.ShapeDtypeStruct((5, K, T), F32), in...  52.6 us
    pallas_call x1, Pallas kernels, per_device(): pl.pallas_call(deliver, out_shape=(jax.ShapeDtypeStruct((1, 3, K, T), F32...  1.34 us

profile of v4, /device:TPU:1, one launch (start us, length us, event | category | flops | bytes accessed | tf_op | source)
XLA Modules:
  0.0 55.2 jit_solution(1798154553316827134)
XLA Ops:
  1.3 52.6 %green_kubo.1.held = f32[5,8,128]{2,1,0:T(8,128)} custom-call(bf16[1536,128]{1,0:T(8,128)(2,1)} %vel.1, bf16[1536,384]{1,0:T(8,128)(2,1)} %vir.1, bf16[384,384]{1,0:T(8,128)(2,1)} %gho.1, bf16[1536,1024]{1,0:T(8,128)(2,1)} %eig.1, s32[1,128]{1,0:T(1,128)} %bitcast.3, s32[1]{0:T(128)S(6)} %copy.9.counts), custom_call_target="tpu_custom_call" | custom-call | tf_op jit(solution)/shard_map/green_kubo/pallas_call | solution.py:364
  53.9 1.3 %deliver.1 = (f32[1,3,8,128]{3,2,1,0:T(8,128)}, f32[1,8,64]{2,1,0:T(8,128)}, f32[1,64]{1,0:T(1,128)}) custom-call(f32[5,8,128]{2,1,0:T(8,128)} %green_kubo.1.held), custom_call_target="tpu_custom_call" | custom-call | tf_op jit(solution)/shard_map/deliver/pallas_call | solution.py:375

commit v5 on v4

--- a/solution.py
+++ b/solution.py
@@ -11,6 +11,8 @@
 MESH = pl.DeviceIdType.MESH
 F32 = jnp.float32
 BF16 = jnp.bfloat16
+I16 = jnp.int16
+TOP = 32767.0
 HIGHEST = lax.Precision.HIGHEST
 NY, NH, NX, NC, NM = 8, 2, 4, 2, 4
 T = 128
@@ -42,6 +44,30 @@
     return jnp.where(iota((FACE, FACE), 0) == target[0:1, :], 1.0, 0.0).astype(BF16)
 
 
+def scale_of(rows):
+    top = jnp.max(jnp.abs(rows), axis=0, keepdims=True)
+    step = jnp.maximum(top, 1e-30) * (1.0 / TOP)
+    e = jnp.floor(jnp.log2(step)) - 13.0
+    return e, jnp.minimum(jnp.ceil(step * jnp.exp2(-e)), TOP)
+
+
+def code(rows, scale):
+    e, f = scale
+    scaled = jnp.clip(jnp.round(rows * (jnp.exp2(-e) / f)), -TOP, TOP)
+    return scaled.astype(jnp.int32).astype(I16)
+
+
+def code_of(scale):
+    e, f = (jnp.broadcast_to(part, (8, T)) for part in scale)
+    return jnp.concatenate([e, f], axis=0).astype(jnp.int32).astype(I16)
+
+
+def decode(coded):
+    count = coded.shape[0] - 16
+    scale = coded[count:].astype(jnp.int32).astype(F32)
+    return coded[:count].astype(jnp.int32).astype(F32) * (jnp.exp2(scale[0:1]) * scale[8:9])
+
+
 def hankel(total):
     parts = []
     for b in range(3):
@@ -83,7 +109,7 @@
 
 def kernel(
     vel, vir, gho, eig, slots, counts, out,
-    ev, ms, nv, rs, gh, ep, vp, part, cr, cs,
+    ev, ms, nv, rs, gh, ep, vp, part, cr, cs, qx, qy, qh,
     rx, x1, ry, rr, rh, ryb, y1b, rxb, rhc, h1c, rxc, x1c, ryc,
     tp, tc, tx, ty, th, sz, sp,
     load_sem, sems, relay,
@@ -199,6 +225,35 @@
             own = own + slots_of[n]
         return own
 
+    def code_over_x(i):
+        block = cs[2 * i]
+        scale = scale_of(block.reshape(512, T))
+        for xx in range(NX):
+            qx[i, xx, 0:128] = code(block[:, :, xx].reshape(128, T), scale)
+            qx[i, xx, 128:144] = code_of(scale)
+        return over_x(qx.at[i], rx.at[i], lambda ref, xx: ref.at[xx])
+
+    def code_over_y():
+        block = cs[1].reshape(512, T)
+        scale = scale_of(block)
+        qy[:, 0:64] = code(block, scale).reshape(NY, 64, T)
+        for yy in range(NY):
+            qy[yy, 64:80] = code_of(scale)
+        return over_y(qy, ryb)
+
+    def code_over_h():
+        block = cs[3, :, 1 - h].reshape(256, T)
+        scale = scale_of(block)
+        qh[0:256] = code(block, scale)
+        qh[256:272] = code_of(scale)
+        return over_h(qh, rhc)
+
+    def gather_coded(copies, own, slots_of):
+        copies.arrive(slots_of)
+        for n in range(slots_of.shape[0]):
+            own = own + decode(slots_of[n])
+        return own
+
     core_send(0)
     told(1)
     tell(2)
@@ -210,7 +265,7 @@
         ep[rows, :] = dot_rows(put, ev[rows, :]).astype(BF16)
         vp[rows, :] = dot_rows(put, ms[rows, 0:T]).astype(BF16)
     core_sum(0)
-    xs0 = over_x(cs.at[0], rx.at[0], lambda ref, xx: ref.at[:, :, xx])
+    xs0 = code_over_x(0)
     told(2)
 
     def add_ghosts(b):
@@ -225,12 +280,12 @@
     add_ghosts(3)
     add_ghosts(1)
     core_sum(3)
-    hsc = over_h(cs.at[3, :, 1 - h], rhc)
+    hsc = code_over_h()
     add_ghosts(2)
     core_sum(1)
-    ysb = over_y(cs.at[1], ryb)
+    ysb = code_over_y()
     core_sum(2)
-    xs2 = over_x(cs.at[2], rx.at[1], lambda ref, xx: ref.at[:, :, xx])
+    xs2 = code_over_x(1)
 
     total = dot_rows(ms[:, :T], ms[:, T:])
     diagonal = iota((T, T), 0) == iota((T, T), 1)
@@ -242,7 +297,7 @@
     tot_core = group()
     tot_core.put(tp, tc, core)
 
-    x1[0] = gather(xs0, cs[0, :, :, x], rx.at[0])
+    x1[0] = gather_coded(xs0, cs[0, :, :, x].reshape(128, T), rx.at[0]).reshape(NY, NH, K, T)
     ys0 = over_y(x1.at[0], ry.at[0])
     tot_core.arrive(tc)
     tx[x] = tp[...] + tc[...]
@@ -250,16 +305,16 @@
     for xx in x_peers:
         tot_x.put(tx.at[x], tx.at[x], dev(x=xx))
     hsc.arrive(rhc)
-    h1c[...] = cs[3, :, h] + rhc[...]
+    h1c[...] = cs[3, :, h] + decode(rhc[...]).reshape(NY, NX, K, T)
     xsc = over_x(h1c, rxc, lambda ref, xx: ref.at[:, xx])
-    x1[1] = gather(xs2, cs[2, :, :, x], rx.at[1])
+    x1[1] = gather_coded(xs2, cs[2, :, :, x].reshape(128, T), rx.at[1]).reshape(NY, NH, K, T)
     ys2 = over_y(x1.at[1], ry.at[1])
     tot_x.arrive(tx.at[pl.ds(0, 3)])
     ty[y] = ((tx[0] + tx[1]) + tx[2]) + tx[3]
     tot_y = group()
     for yy in y_peers:
         tot_y.put(ty.at[y], ty.at[y], dev(y=yy))
-    y1b[...] = gather(ysb, cs[1, y], ryb)
+    y1b[...] = gather_coded(ysb, cs[1, y].reshape(64, T), ryb).reshape(NH, NX, K, T)
     xsb = over_x(y1b, rxb, lambda ref, xx: ref.at[:, xx])
     x1c[...] = gather(xsc, h1c[:, x], rxc)
     ysc = over_y(x1c, ryc)
@@ -275,8 +330,6 @@
     hs2 = over_h(rr.at[2, 1 - h], rh.at[2])
     rr[1] = gather(xsb, y1b[:, x], rxb)
     hs1 = over_h(rr.at[1, 1 - h], rh.at[1])
-    tot_h.arrive(th.at[1])
-    lagged = hankel((th[0] + th[1]) * (1.0 / math.sqrt(ms.shape[0] // 3 * domains)))
     last = gather(ysc, x1c[y], ryc)
     hs0.arrive(rh.at[0])
     hs2.arrive(rh.at[2])
@@ -289,6 +342,8 @@
     szs = group()
     for zz, cc in z_peers:
         szs.put(sz.at[here], sz.at[here], dev(h=lax.div(zz, NM), m=lax.rem(zz, NM), c=cc))
+    tot_h.arrive(th.at[1])
+    lagged = hankel((th[0] + th[1]) * (1.0 / math.sqrt(ms.shape[0] // 3 * domains)))
     for b in range(3):
         out[b] = flux[:, b * T : (b + 1) * T]
     out[3] = correlate(flux, lagged)
@@ -337,15 +392,18 @@
         vmem((4, NY, NH, NX, NC, K, T), F32),
         vmem((4, NY, NH, NX, K, T), F32),
         vmem((4, NY, NH, NX, K, T), F32),
-        vmem((2, 3, NY, NH, K, T), F32),
+        vmem((2, NX, 144, T), I16),
+        vmem((NY, 80, T), I16),
+        vmem((272, T), I16),
+        vmem((2, 3, 144, T), I16),
         vmem((2, NY, NH, K, T), F32),
         vmem((2, NY - 1, NH, K, T), F32),
         vmem((3, NH, K, T), F32),
         vmem((3, K, T), F32),
-        vmem((NY - 1, NH, NX, K, T), F32),
+        vmem((NY - 1, 80, T), I16),
         vmem((NH, NX, K, T), F32),
         vmem((3, NH, K, T), F32),
-        vmem((NY, NX, K, T), F32),
+        vmem((272, T), I16),
         vmem((NY, NX, K, T), F32),
         vmem((3, NY, K, T), F32),
         vmem((NY, K, T), F32),

time: 55.4 us -> 52 us (0.939)
  Pallas kernels: 53.9 us -> 50.6 us
    pallas_call x1, Pallas kernels: 52.6 us -> 49.2 us  [per_device(): pl.pallas_call(kernel, out_shape=jax.ShapeDtypeStruct((5, K, T), F32), in...]
where the time goes in v5:
time: 52 us; the launch traced here: 51.9 us
  Pallas kernels  50.6 us (97%)
  between operations  1.29 us (2%)
    pallas_call x1, Pallas kernels, per_device(): pl.pallas_call(kernel, out_shape=jax.ShapeDtypeStruct((5, K, T), F32), in...  49.2 us
    pallas_call x1, Pallas kernels, per_device(): pl.pallas_call(deliver, out_shape=(jax.ShapeDtypeStruct((1, 3, K, T), F32...  1.34 us

profile of v5, /device:TPU:1, one launch (start us, length us, event | category | flops | bytes accessed | tf_op | source)
XLA Modules:
  0.0 51.9 jit_solution(2606116871207176298)
XLA Ops:
  1.3 49.2 %green_kubo.1.held = f32[5,8,128]{2,1,0:T(8,128)} custom-call(bf16[1536,128]{1,0:T(8,128)(2,1)} %vel.1, bf16[1536,384]{1,0:T(8,128)(2,1)} %vir.1, bf16[384,384]{1,0:T(8,128)(2,1)} %gho.1, bf16[1536,1024]{1,0:T(8,128)(2,1)} %eig.1, s32[1,128]{1,0:T(1,128)} %bitcast.3, s32[1]{0:T(128)S(6)} %copy.9.counts), custom_call_target="tpu_custom_call" | custom-call | tf_op jit(solution)/shard_map/green_kubo/pallas_call | solution.py:422
  50.5 1.3 %deliver.1 = (f32[1,3,8,128]{3,2,1,0:T(8,128)}, f32[1,8,64]{2,1,0:T(8,128)}, f32[1,64]{1,0:T(1,128)}) custom-call(f32[5,8,128]{2,1,0:T(8,128)} %green_kubo.1.held), custom_call_target="tpu_custom_call" | custom-call | tf_op jit(solution)/shard_map/deliver/pallas_call | solution.py:433

commit v6 on v5

--- a/solution.py
+++ b/solution.py
@@ -20,6 +20,7 @@
 FACE = 192
 LAGS = 64
 RING = (4, 3, 5, 2, 6, 1, 7)
+HX = ((1, 2), (1, 1), (1, 3), (1, 0), (0, 2), (0, 1), (0, 3))
 
 
 def dot_rows(left, right):
@@ -126,6 +127,7 @@
     core = dev(c=1 - c)
     h_peer = dev(h=1 - h)
     x_peers = [lax.rem(x + k, NX) for k in (2, 1, 3)]
+    hx_peers = [(lax.rem(h + i, NH), lax.rem(x + k, NX)) for i, k in HX]
     y_peers = [lax.rem(y + k, NY) for k in RING]
     z_peers = [(lax.rem(z + k, 8), lax.rem(c + i, NC)) for k in RING for i in (1, 0)] + [(z, 1 - c)]
     steps = sorted(range(1, 32), key=lambda i: -min(i // 4, NY - i // 4) - min(i % 4, NX - i % 4))
@@ -169,7 +171,7 @@
     places[0].put(slots, rs.at[0], above)
     places[1].put(slots, rs.at[1], below)
     ghost_copies = {}
-    for b in (2, 0, 1):
+    for b in (2, 1, 0):
         cols = pl.ds(b * T, T)
         for side, device in enumerate((above, below)):
             ghost_copies[b, side] = group()
@@ -267,6 +269,7 @@
     core_sum(0)
     xs0 = code_over_x(0)
     told(2)
+    pl.semaphore_signal(relay.at[3], 1, device_id=h_peer, device_id_type=MESH)
 
     def add_ghosts(b):
         for side in range(2):
@@ -278,14 +281,14 @@
         core_send(b)
 
     add_ghosts(3)
-    add_ghosts(1)
+    add_ghosts(2)
     core_sum(3)
     hsc = code_over_h()
-    add_ghosts(2)
+    add_ghosts(1)
+    core_sum(2)
+    xs2 = code_over_x(1)
     core_sum(1)
     ysb = code_over_y()
-    core_sum(2)
-    xs2 = code_over_x(1)
 
     total = dot_rows(ms[:, :T], ms[:, T:])
     diagonal = iota((T, T), 0) == iota((T, T), 1)
@@ -304,18 +307,21 @@
     tot_x = group()
     for xx in x_peers:
         tot_x.put(tx.at[x], tx.at[x], dev(x=xx))
+    x1[1] = gather_coded(xs2, cs[2, :, :, x].reshape(128, T), rx.at[1]).reshape(NY, NH, K, T)
+    ys2 = over_y(x1.at[1], ry.at[1])
     hsc.arrive(rhc)
     h1c[...] = cs[3, :, h] + decode(rhc[...]).reshape(NY, NX, K, T)
     xsc = over_x(h1c, rxc, lambda ref, xx: ref.at[:, xx])
-    x1[1] = gather_coded(xs2, cs[2, :, :, x].reshape(128, T), rx.at[1]).reshape(NY, NH, K, T)
-    ys2 = over_y(x1.at[1], ry.at[1])
     tot_x.arrive(tx.at[pl.ds(0, 3)])
     ty[y] = ((tx[0] + tx[1]) + tx[2]) + tx[3]
     tot_y = group()
     for yy in y_peers:
         tot_y.put(ty.at[y], ty.at[y], dev(y=yy))
     y1b[...] = gather_coded(ysb, cs[1, y].reshape(64, T), ryb).reshape(NH, NX, K, T)
-    xsb = over_x(y1b, rxb, lambda ref, xx: ref.at[:, xx])
+    pl.semaphore_wait(relay.at[3], 1)
+    xsb = group()
+    for n, (hh, xx) in enumerate(hx_peers):
+        xsb.put(y1b.at[hh, xx], rxb.at[n], dev(h=hh, x=xx))
     x1c[...] = gather(xsc, h1c[:, x], rxc)
     ysc = over_y(x1c, ryc)
     rr[0] = gather(ys0, x1[0, y], ry.at[0])
@@ -326,15 +332,12 @@
         summed = summed + ty[n]
     th[0] = summed
     tot_h = over_h(th.at[0], th.at[1])
-    rr[2] = gather(ys2, x1[1, y], ry.at[1])
-    hs2 = over_h(rr.at[2, 1 - h], rh.at[2])
-    rr[1] = gather(xsb, y1b[:, x], rxb)
-    hs1 = over_h(rr.at[1, 1 - h], rh.at[1])
+    rr[1] = gather(ys2, x1[1, y], ry.at[1])
+    hs2 = over_h(rr.at[1, 1 - h], rh.at[1])
     last = gather(ysc, x1c[y], ryc)
     hs0.arrive(rh.at[0])
-    hs2.arrive(rh.at[2])
-    hs1.arrive(rh.at[1])
-    final = [rr[b, h] + rh[b] for b in range(3)] + [last]
+    hs2.arrive(rh.at[1])
+    final = [rr[0, h] + rh[0], gather(xsb, y1b[h, x], rxb), rr[1, h] + rh[1], last]
     flux = jnp.concatenate([final[0] * final[1 + b] for b in range(3)], axis=1)
 
     here = z * NC + c
@@ -349,7 +352,7 @@
     out[3] = correlate(flux, lagged)
     for copies in places + list(ghost_copies.values()) + list(cores.values()):
         copies.left()
-    for copies in (xs0, ys0, hs0, ysb, xsb, hs1, xs2, ys2, hs2, hsc, xsc, ysc):
+    for copies in (xs0, ys0, hs0, ysb, xsb, xs2, ys2, hs2, hsc, xsc, ysc):
         copies.left()
     for copies in (tot_core, tot_x, tot_y, tot_h):
         copies.left()
@@ -398,11 +401,11 @@
         vmem((2, 3, 144, T), I16),
         vmem((2, NY, NH, K, T), F32),
         vmem((2, NY - 1, NH, K, T), F32),
-        vmem((3, NH, K, T), F32),
-        vmem((3, K, T), F32),
+        vmem((2, NH, K, T), F32),
+        vmem((2, K, T), F32),
         vmem((NY - 1, 80, T), I16),
         vmem((NH, NX, K, T), F32),
-        vmem((3, NH, K, T), F32),
+        vmem((7, K, T), F32),
         vmem((272, T), I16),
         vmem((NY, NX, K, T), F32),
         vmem((3, NY, K, T), F32),
@@ -417,7 +420,7 @@
         vmem((32, 1, 3 * T), F32),
         dma((7,)),
         dma((2, 32)),
-        pltpu.SemaphoreType.REGULAR((3,)),
+        pltpu.SemaphoreType.REGULAR((4,)),
     ]
     held = pl.pallas_call(
         kernel,

time: 52 us -> 51.9 us (level)
  no operation moved by 1% of the time
where the time goes in v6:
time: 51.9 us; the launch traced here: 51.7 us
  Pallas kernels  50.4 us (97%)
  between operations  1.29 us (2%)
    pallas_call x1, Pallas kernels, per_device(): pl.pallas_call(kernel, out_shape=jax.ShapeDtypeStruct((5, K, T), F32), in...  49.1 us
    pallas_call x1, Pallas kernels, per_device(): pl.pallas_call(deliver, out_shape=(jax.ShapeDtypeStruct((1, 3, K, T), F32...  1.34 us

profile of v6, /device:TPU:1, one launch (start us, length us, event | category | flops | bytes accessed | tf_op | source)
XLA Modules:
  0.0 51.7 jit_solution(5608968024296371822)
XLA Ops:
  1.3 49.1 %green_kubo.1.held = f32[5,8,128]{2,1,0:T(8,128)} custom-call(bf16[1536,128]{1,0:T(8,128)(2,1)} %vel.1, bf16[1536,384]{1,0:T(8,128)(2,1)} %vir.1, bf16[384,384]{1,0:T(8,128)(2,1)} %gho.1, bf16[1536,1024]{1,0:T(8,128)(2,1)} %eig.1, s32[1,128]{1,0:T(1,128)} %bitcast.3, s32[1]{0:T(128)S(6)} %copy.9.counts), custom_call_target="tpu_custom_call" | custom-call | tf_op jit(solution)/shard_map/green_kubo/pallas_call | solution.py:425
  50.4 1.3 %deliver.1 = (f32[1,3,8,128]{3,2,1,0:T(8,128)}, f32[1,8,64]{2,1,0:T(8,128)}, f32[1,64]{1,0:T(1,128)}) custom-call(f32[5,8,128]{2,1,0:T(8,128)} %green_kubo.1.held), custom_call_target="tpu_custom_call" | custom-call | tf_op jit(solution)/shard_map/deliver/pallas_call | solution.py:436
